TPU v7x, 32 devices: a whole 2x2x4 slice. The times are simulated.
32 devices in a mesh: dp: 8 (over z, y), mp: 4 (over x, core).
Axes of the slice: x: 2, y: 2, z: 4, core: 2. Of those that a mesh axis runs over, the one named last changes fastest.
Arguments:
- hidden: bfloat16 [24576, 1024], P('dp', 'mp'), may hold values from -6 to 6
- first_gain: float32 [1024], replicated, may hold values from 0.25 to 1.75
- first_bias: float32 [1024], replicated, may hold values from -1.5 to 1.5
- second_gain: float32 [1024], replicated, may hold values from 0.25 to 1.75
- second_bias: float32 [1024], replicated, may hold values from -1.5 to 1.5
- joined_frozen_weight: bfloat16 [1024, 3072], P(None, 'mp'), may hold values from -0.1875 to 0.1875
- output_frozen_weight: bfloat16 [1024, 1024], P(None, 'mp'), may hold values from -1.5 to 1.5
- expand_frozen_weight: bfloat16 [1024, 4096], P(None, 'mp'), may hold values from -0.1875 to 0.1875
- shrink_frozen_weight: bfloat16 [4096, 1024], P(None, 'mp'), may hold values from -0.09375 to 0.09375
- joined_a: bfloat16 [1024, 128], replicated, may hold values from -0.1875 to 0.1875
- joined_up_factor: bfloat16 [128, 3072], replicated, may hold values from -0.5 to 0.5
- output_a: bfloat16 [1024, 128], replicated, may hold values from -0.1875 to 0.1875
- output_up_factor: bfloat16 [128, 1024], replicated, may hold values from -2 to 2
- expand_a: bfloat16 [1024, 128], replicated, may hold values from -0.1875 to 0.1875
- expand_up_factor: bfloat16 [128, 4096], replicated, may hold values from -0.5 to 0.5
- shrink_a: bfloat16 [4096, 128], replicated, may hold values from -0.09375 to 0.09375
- shrink_up_factor: bfloat16 [128, 1024], replicated, may hold values from -0.5 to 0.5
- cotangent: bfloat16 [24576, 1024], P('dp', 'mp'), may hold values from -6 to 6
Outputs:
- result: bfloat16 [24576, 1024], P('dp', 'mp')
- hidden_grad: float32 [24576, 1024], P('dp', 'mp')
- first_gain_grad: float32 [1024], replicated
- first_bias_grad: float32 [1024], replicated
- second_gain_grad: float32 [1024], replicated
- second_bias_grad: float32 [1024], replicated
- joined_a_grad: float32 [1024, 128], replicated
- joined_b_grad: float32 [128, 3072], replicated
- output_a_grad: float32 [1024, 128], replicated
- output_b_grad: float32 [128, 1024], replicated
- expand_a_grad: float32 [1024, 128], replicated
- expand_b_grad: float32 [128, 4096], replicated
- shrink_a_grad: float32 [4096, 128], replicated
- shrink_b_grad: float32 [128, 1024], replicated
All inputs are finite; a program needn't handle non-finite values.
Results may differ from a plain program's by a relative error of at most 0.0045.
The roundings to bfloat16 on the way count: a program that leaves them out, or rounds other values in their place, can miss the bound.
Values may be sent and summed in bfloat16 or wider, within the bound.
No kernel may reach another device: no remote copies, remote signals or barrier semaphores. Data moves between devices by JAX's collectives and lax.ppermute only.
A program may use at most 384 MiB of HBM per device.

v0:
```python
from functools import partial

import jax
import jax.numpy as jnp
from jax import lax
from jax.sharding import PartitionSpec as P

ROTARY = 16
SEQ_LEN = 1024
HEAD_DIM = 64


ADAPTER_SCALE = 0.25
EPS = 1e-05


def matrix_product(left, right):
    return jnp.dot(left, right, preferred_element_type=jnp.float32)


def matrix_product_transposed_left(left, right):
    return lax.dot_general(
        left, right, (((0,), (0,)), ((), ())), preferred_element_type=jnp.float32
    )


def matrix_product_transposed_right(left, right):
    return lax.dot_general(
        left, right, (((1,), (1,)), ((), ())), preferred_element_type=jnp.float32
    )


def normalize(full, gain, bias):
    center = full - jnp.mean(full, -1, keepdims=True)
    factor = lax.rsqrt(jnp.mean(center * center, -1, keepdims=True) + EPS)
    unit = center * factor
    return (unit, factor, unit * gain + bias)


def tables():
    position = jnp.arange(SEQ_LEN, dtype=jnp.float32)[:, None]
    frequency = 10000.0 ** (-(jnp.arange(ROTARY // 2, dtype=jnp.float32) * 2.0) / ROTARY)
    angles = position * frequency[None, :]
    cosine = jnp.concatenate([jnp.cos(angles), jnp.cos(angles)], -1)[:, None, :]
    sine = jnp.concatenate([jnp.sin(angles), jnp.sin(angles)], -1)[:, None, :]
    return (cosine, sine)


def rotate(block, cosine, sine):
    half = ROTARY // 2
    part = block[..., :ROTARY]
    turned = jnp.concatenate([-part[..., half:], part[..., :half]], -1)
    return jnp.concatenate([part * cosine + turned * sine, block[..., ROTARY:]], -1)


def unrotate(grad, cosine, sine):
    half = ROTARY // 2
    part = grad[..., :ROTARY]
    scaled = part * sine
    untied = jnp.concatenate([scaled[..., half:], -scaled[..., :half]], -1)
    return jnp.concatenate([part * cosine + untied, grad[..., ROTARY:]], -1)


def attend(causal, block):
    query, keys, values = block
    scores = jnp.einsum(
        "qhe,khe->hqk", query, keys, preferred_element_type=jnp.float32
    ) * HEAD_DIM ** (-0.5)
    scores = jnp.where(causal, scores, -1e30)
    peak = jnp.max(scores, -1, keepdims=True)
    weights = jnp.exp(scores - peak)
    total = jnp.sum(weights, -1, keepdims=True)
    probs = (weights / total).astype(jnp.bfloat16)
    attended_context = jnp.einsum("hqk,khe->qhe", probs, values, preferred_element_type=jnp.float32)
    return (attended_context.astype(jnp.bfloat16), (peak + jnp.log(total))[..., 0])


def attend_back(causal, block):
    query, keys, values, grad_context, logsum = block
    scores = jnp.einsum(
        "qhe,khe->hqk", query, keys, preferred_element_type=jnp.float32
    ) * HEAD_DIM ** (-0.5)
    scores = jnp.where(causal, scores, -1e30)
    probs = jnp.exp(scores - logsum[..., None])
    grad_probs = jnp.einsum(
        "qhe,khe->hqk", grad_context, values, preferred_element_type=jnp.float32
    )
    inner = jnp.sum(probs * grad_probs, -1, keepdims=True)
    grad_scores = (probs * (grad_probs - inner)).astype(jnp.bfloat16)
    grad_query = jnp.einsum(
        "hqk,khe->qhe", grad_scores, keys, preferred_element_type=jnp.float32
    ) * HEAD_DIM ** (-0.5)
    grad_keys = jnp.einsum(
        "hqk,qhe->khe", grad_scores, query, preferred_element_type=jnp.float32
    ) * HEAD_DIM ** (-0.5)
    grad_values = jnp.einsum(
        "hqk,qhe->khe", probs.astype(jnp.bfloat16), grad_context, preferred_element_type=jnp.float32
    )
    return (grad_query, grad_keys, grad_values)


def fold_with(weight, adapter_a, carry, piece):
    span = piece.shape[1]
    weight_rows = lax.slice_in_dim(weight, 0, span, axis=0)
    adapter_rows = lax.slice_in_dim(adapter_a, 0, span, axis=0)
    return (
        carry[0] + matrix_product(piece, weight_rows),
        carry[1] + matrix_product(piece, adapter_rows),
    )


def finish(summed_result, low_sum, columns_up_factor):
    adapter_values = low_sum.astype(jnp.bfloat16)
    return (
        summed_result + ADAPTER_SCALE * matrix_product(adapter_values, columns_up_factor),
        adapter_values,
    )


def on_device(
    hidden,
    first_gain,
    first_bias,
    second_gain,
    second_bias,
    joined_frozen_weight,
    output_frozen_weight,
    expand_frozen_weight,
    shrink_frozen_weight,
    joined_a,
    joined_up_factor,
    output_a,
    output_up_factor,
    expand_a,
    expand_up_factor,
    shrink_a,
    shrink_up_factor,
    cotangent,
):
    rank = lax.axis_index("mp")
    rows = hidden.shape[0]
    cols = hidden.shape[1]
    width = cols * lax.axis_size("mp")
    count = rows // SEQ_LEN
    joined_cols = joined_frozen_weight.shape[1]
    expand_cols = expand_frozen_weight.shape[1]
    heads_here = joined_cols // (3 * HEAD_DIM)
    inner_out = joined_cols // 3
    full = lax.all_gather(hidden, "mp", axis=1, tiled=True).astype(jnp.float32)
    unit_one, factor_one, first_norm_output = normalize(full, first_gain, first_bias)
    unit_two, factor_two, second_norm_output = normalize(full, second_gain, second_bias)
    first_norm_output = first_norm_output.astype(jnp.bfloat16)
    second_norm_output = second_norm_output.astype(jnp.bfloat16)
    adapter_joined_hidden = matrix_product(first_norm_output, joined_a).astype(jnp.bfloat16)
    joined_weight_local = lax.dynamic_slice_in_dim(
        joined_up_factor, rank * joined_cols, joined_cols, 1
    )
    mixed_state = matrix_product(
        first_norm_output, joined_frozen_weight
    ) + ADAPTER_SCALE * matrix_product(adapter_joined_hidden, joined_weight_local)
    mixed_state = mixed_state.reshape(count, SEQ_LEN, heads_here, 3, HEAD_DIM)
    cosine, sine = tables()
    query = rotate(mixed_state[:, :, :, 0], cosine, sine).astype(jnp.bfloat16)
    keys = rotate(mixed_state[:, :, :, 1], cosine, sine).astype(jnp.bfloat16)
    values = mixed_state[:, :, :, 2].astype(jnp.bfloat16)
    causal = jnp.arange(SEQ_LEN)[:, None] >= jnp.arange(SEQ_LEN)[None, :]
    attended_context, logsum = lax.map(partial(attend, causal), (query, keys, values))
    attended_context = attended_context.reshape(rows, inner_out)
    adapter_expand_hidden = matrix_product(second_norm_output, expand_a).astype(jnp.bfloat16)
    expand_weight_local = lax.dynamic_slice_in_dim(
        expand_up_factor, rank * expand_cols, expand_cols, 1
    )
    upper_hidden = matrix_product(
        second_norm_output, expand_frozen_weight
    ) + ADAPTER_SCALE * matrix_product(adapter_expand_hidden, expand_weight_local)
    gelu_exact = partial(jax.nn.gelu, approximate=False)
    active_f, gelu_pull = jax.vjp(gelu_exact, upper_hidden)
    active_hidden = active_f.astype(jnp.bfloat16)
    out_rows_a = lax.dynamic_slice_in_dim(output_a, rank * inner_out, inner_out, 0)
    output_columns_up_factor = lax.dynamic_slice_in_dim(output_up_factor, rank * cols, cols, 1)
    shrink_rows_a = lax.dynamic_slice_in_dim(shrink_a, rank * expand_cols, expand_cols, 0)
    shrink_columns_up_factor = lax.dynamic_slice_in_dim(shrink_up_factor, rank * cols, cols, 1)
    zero_pair = (
        jnp.zeros((rows, cols), jnp.float32),
        jnp.zeros((rows, output_a.shape[1]), jnp.float32),
    )
    attn_summed, attn_low = fold_with(
        output_frozen_weight,
        output_a,
        zero_pair,
        lax.all_gather(attended_context, "mp", axis=1, tiled=True),
    )
    mlp_summed, mlp_low = fold_with(
        shrink_frozen_weight,
        shrink_a,
        zero_pair,
        jax.tree.map(lambda a: lax.all_gather(a, "mp", axis=1, tiled=True), active_hidden),
    )
    attention_branch, adapter_output_hidden = finish(
        attn_summed, attn_low, output_columns_up_factor
    )
    feedforward_branch, adapter_shrink_hidden = finish(
        mlp_summed, mlp_low, shrink_columns_up_factor
    )
    result = (hidden.astype(jnp.float32) + attention_branch + feedforward_branch).astype(
        jnp.bfloat16
    )
    back_out, back_shrink = (
        lax.psum_scatter(
            matrix_product_transposed_right(cotangent, output_frozen_weight),
            "mp",
            scatter_dimension=1,
            tiled=True,
        ),
        lax.psum_scatter(
            matrix_product_transposed_right(cotangent, shrink_frozen_weight),
            "mp",
            scatter_dimension=1,
            tiled=True,
        ),
    )
    rank_out, rank_shrink = lax.psum(
        (
            ADAPTER_SCALE * matrix_product_transposed_right(cotangent, output_columns_up_factor),
            ADAPTER_SCALE * matrix_product_transposed_right(cotangent, shrink_columns_up_factor),
        ),
        "mp",
    )
    low_out_grad = rank_out.astype(jnp.bfloat16)
    low_shrink_grad = rank_shrink.astype(jnp.bfloat16)
    output_up_factor_piece = ADAPTER_SCALE * matrix_product_transposed_left(
        adapter_output_hidden, cotangent
    )
    shrink_up_factor_piece = ADAPTER_SCALE * matrix_product_transposed_left(
        adapter_shrink_hidden, cotangent
    )
    grad_context = (back_out + matrix_product_transposed_right(low_out_grad, out_rows_a)).astype(
        jnp.bfloat16
    )
    output_a_piece = matrix_product_transposed_left(attended_context, low_out_grad)
    shrink_a_piece = matrix_product_transposed_left(active_hidden, low_shrink_grad)
    grad_active = back_shrink + matrix_product_transposed_right(low_shrink_grad, shrink_rows_a)
    upper_gradient = gelu_pull(grad_active)[0].astype(jnp.bfloat16)
    grad_context = grad_context.reshape(count, SEQ_LEN, heads_here, HEAD_DIM)
    grad_query, grad_keys, grad_values = lax.map(
        partial(attend_back, causal), (query, keys, values, grad_context, logsum)
    )
    mixed_gradient = jnp.stack(
        [unrotate(grad_query, cosine, sine), unrotate(grad_keys, cosine, sine), grad_values], 3
    )
    mixed_gradient = mixed_gradient.reshape(rows, joined_cols).astype(jnp.bfloat16)
    rank_joined, rank_expand = lax.psum(
        (
            ADAPTER_SCALE * matrix_product_transposed_right(mixed_gradient, joined_weight_local),
            ADAPTER_SCALE * matrix_product_transposed_right(upper_gradient, expand_weight_local),
        ),
        "mp",
    )
    low_joined_grad = rank_joined.astype(jnp.bfloat16)
    low_expand_grad = rank_expand.astype(jnp.bfloat16)
    joined_up_factor_piece = ADAPTER_SCALE * matrix_product_transposed_left(
        adapter_joined_hidden, mixed_gradient
    )
    expand_up_factor_piece = ADAPTER_SCALE * matrix_product_transposed_left(
        adapter_expand_hidden, upper_gradient
    )
    norm_one_cols = lax.dynamic_slice_in_dim(first_norm_output, rank * cols, cols, 1)
    norm_two_cols = lax.dynamic_slice_in_dim(second_norm_output, rank * cols, cols, 1)
    joined_a_piece = matrix_product_transposed_left(norm_one_cols, low_joined_grad)
    expand_a_piece = matrix_product_transposed_left(norm_two_cols, low_expand_grad)
    grad_one, grad_two = (
        lax.psum_scatter(
            matrix_product_transposed_right(mixed_gradient, joined_frozen_weight),
            "mp",
            scatter_dimension=1,
            tiled=True,
        ),
        lax.psum_scatter(
            matrix_product_transposed_right(upper_gradient, expand_frozen_weight),
            "mp",
            scatter_dimension=1,
            tiled=True,
        ),
    )
    joined_rows_a = lax.dynamic_slice_in_dim(joined_a, rank * cols, cols, 0)
    expand_rows_a = lax.dynamic_slice_in_dim(expand_a, rank * cols, cols, 0)
    grad_one = grad_one + matrix_product_transposed_right(low_joined_grad, joined_rows_a)
    grad_two = grad_two + matrix_product_transposed_right(low_expand_grad, expand_rows_a)
    unit_one_cols = lax.dynamic_slice_in_dim(unit_one, rank * cols, cols, 1)
    unit_two_cols = lax.dynamic_slice_in_dim(unit_two, rank * cols, cols, 1)
    gain_one_cols = lax.dynamic_slice_in_dim(first_gain, rank * cols, cols, 0)
    gain_two_cols = lax.dynamic_slice_in_dim(second_gain, rank * cols, cols, 0)
    first_gain_piece = jnp.sum(grad_one * unit_one_cols, 0)
    first_bias_piece = jnp.sum(grad_one, 0)
    second_gain_piece = jnp.sum(grad_two * unit_two_cols, 0)
    second_bias_piece = jnp.sum(grad_two, 0)
    scaled_one = grad_one * gain_one_cols
    scaled_two = grad_two * gain_two_cols
    plain_one, along_one, plain_two, along_two = (
        lax.psum(jnp.sum(scaled_one, -1).astype(jnp.bfloat16), "mp").astype(jnp.float32),
        lax.psum(jnp.sum(scaled_one * unit_one_cols, -1).astype(jnp.bfloat16), "mp").astype(
            jnp.float32
        ),
        lax.psum(jnp.sum(scaled_two, -1).astype(jnp.bfloat16), "mp").astype(jnp.float32),
        lax.psum(jnp.sum(scaled_two * unit_two_cols, -1).astype(jnp.bfloat16), "mp").astype(
            jnp.float32
        ),
    )
    back_one = factor_one * (
        scaled_one - plain_one[:, None] / width - unit_one_cols * along_one[:, None] / width
    )
    back_two = factor_two * (
        scaled_two - plain_two[:, None] / width - unit_two_cols * along_two[:, None] / width
    )
    hidden_grad = cotangent.astype(jnp.float32) + back_one + back_two
    pieces = (
        first_gain_piece,
        first_bias_piece,
        second_gain_piece,
        second_bias_piece,
        joined_a_piece,
        joined_up_factor_piece,
        output_a_piece,
        output_up_factor_piece,
        expand_a_piece,
        expand_up_factor_piece,
        shrink_a_piece,
        shrink_up_factor_piece,
    )
    shapes = (
        first_gain.shape,
        first_bias.shape,
        second_gain.shape,
        second_bias.shape,
        joined_a.shape,
        joined_up_factor.shape,
        output_a.shape,
        output_up_factor.shape,
        expand_a.shape,
        expand_up_factor.shape,
        shrink_a.shape,
        shrink_up_factor.shape,
    )
    along = (0, 0, 0, 0, 0, 1, 0, 1, 0, 1, 0, 1)
    padded = [
        lax.dynamic_update_slice_in_dim(
            jnp.zeros(shape, jnp.float32), piece, rank * piece.shape[axis_dim], axis_dim
        )
        for piece, shape, axis_dim in zip(pieces, shapes, along)
    ]
    grads = lax.psum(
        (
            padded[0],
            padded[1],
            padded[2],
            padded[3],
            padded[4],
            padded[5],
            padded[6],
            padded[7],
            padded[8],
            padded[9],
            padded[10],
            padded[11],
        ),
        ("dp", "mp"),
    )
    return (
        result,
        hidden_grad,
        grads[0],
        grads[1],
        grads[2],
        grads[3],
        grads[4],
        grads[5],
        grads[6],
        grads[7],
        grads[8],
        grads[9],
        grads[10],
        grads[11],
    )


def solution(mesh):
    return jax.shard_map(
        on_device,
        mesh=mesh,
        in_specs=(
            P("dp", "mp"),
            P(),
            P(),
            P(),
            P(),
            P(None, "mp"),
            P(None, "mp"),
            P(None, "mp"),
            P(None, "mp"),
            P(),
            P(),
            P(),
            P(),
            P(),
            P(),
            P(),
            P(),
            P("dp", "mp"),
        ),
        out_specs=(
            P("dp", "mp"),
            P("dp", "mp"),
            P(),
            P(),
            P(),
            P(),
            P(),
            P(),
            P(),
            P(),
            P(),
            P(),
            P(),
            P(),
        ),
        check_vma=False,
    )
```

profile of v0, /device:TPU:0, one launch (start us, length us, event | category | flops | bytes accessed | tf_op | source)
XLA Modules:
  0.0 1221.2 jit_solution(1445994409440878774)
XLA Ops:
  15.9 21.8 %fusion.136 = f32[3072,4096]{1,0:T(8,128)} fusion(bf16[3072,256]{1,0:T(8,128)(2,1)} %param.39, bf16[4096,256]{1,0:T(8,128)(2,1)S(1)} %copy-done), kind=kOutput, calls=%fused_computation.213 | convolution fusion | flops 6442450944 | bytes 54001664 | tf_op jit(solution)/shard_map/dot_general | solution.py:28
  38.3 21.2 %all-gather.4.cloned.1.call-done = bf16[3072,1024]{1,0:T(8,128)(2,1)} async-done(((bf16[3072,256]{1,0:T(8,128)(2,1)}), bf16[3072,1024]{1,0:T(8,128)(2,1)}) %all-gather.4.cloned.1.call-update) | async-done | bytes 6291472 | tf_op jit(solution)/shard_map/all_gather | solution.py:149
  66.3 10.8 fusion.53
  101.4 16.3 %reshape.99 = f32[3,1024,4,3,64]{1,0,4,3,2:T(4,128)} reshape(f32[3072,768]{0,1:T(8,128)} %copy.44) | data formatting | bytes 18874368 | tf_op jit(solution)/shard_map/reshape | solution.py:161
  139.5 47.4 %while.28 = (s32[]{:T(128)}, bf16[3,1024,4,64]{1,3,2,0:T(8,128)(2,1)}, f32[3,4,1024]{2,1,0:T(4,128)S(1)}, bf16[3,1024,4,64]{1,3,2,0:T(8,128)(2,1)}, bf16[3,1024,...) while((s32[]{:T(128)}, bf16[3,1024,4,64]{1,3,2,0:T(8,128)(2,1)}, ...), condition=%wide.region_5.6_spmd.clone, body=%wide.region_2.5_spmd.clone.sunk | while | flops 1125380096 | bytes 69339280 | solution.py:167
  194.3 11.2 fusion.132
  205.5 32.4 %multiply_convert_fusion.1 = (bf16[3072,1024]{1,0:T(8,128)(2,1)}, f32[3072,1024]{1,0:T(8,128)}, f32[3072,1024]{1,0:T(8,128)}) fusion(f32[3072,1024]{1,0:T(8,128)S(1)} %fusion.132, bf16[3072,128]{1,0:T(8,128)(2,1)S(1)} %convolution_convert_fusion, bf16[128,4096]{1,0:T(8,128)(2,1)} %param.36, s32[]{:T(128)S(6)} %select_n.15), kind=kOutput, calls=%fused_computation.67 | convolution fusion | flops 1016070144 | bytes 45088772 | tf_op jit(solution)/shard_map/dot_general | solution.py:18
  244.5 110.5 %all-reduce.10 = (bf16[3072,128]{0,1:T(8,128)(2,1)}, bf16[3072,128]{0,1:T(8,128)(2,1)S(1)}) all-reduce(f32[3072,128]{0,1:T(8,128)} %fusion.68, f32[3072,128]{0,1:T(8,128)} %fusion.69), channel_id=1, replica_groups=mesh['dp'=8,'mp'=4] {'mp'}, use_global_device_ids=true, to_apply=%region_18.19 | all-reduce | flops 786432 | bytes 4718592 | tf_op jit(solution)/shard_map/psum | solution.py:222
  370.3 173.2 %while.29 = (s32[]{:T(128)}, f32[3,1024,4,64]{1,3,2,0:T(8,128)}, f32[3,1024,4,64]{1,3,2,0:T(8,128)}, bf16[3,1024,4,64]{1,3,2,0:T(8,128)(2,1)}, bf16[3,1024,4,64]...) while((s32[]{:T(128)}, f32[3,1024,4,64]{1,3,2,0:T(8,128)}, ...), condition=%wide.region_10.11_spmd.clone, body=%wide.region_8.10_spmd.clone.sunk | while | flops 2723672064 | bytes 235492544 | solution.py:245
  380.3 13.2 %multiply_reduce_fusion.8 = (f32[4,1024]{1,0:T(4,128)S(1)}, f32[4,1024,1024]{1,2,0:T(8,128)}) fusion(f32[4,1024,1024]{1,2,0:T(8,128)} %fusion.218, f32[4,1024]{1,0:T(4,128)S(1)} %dynamic-slice_bitcast_fusion.2, bf16[3,1024,4,64]{1,3,2,0:T(8,128)(2,1)} %get-tuple-element.407, s32[]{:T(128)S(6)} %copy.89, ...), kind=kOutput, calls=%fused_computation.25.clone.1 | convolution fusion | flops 557838336 | bytes 35685376 | tf_op jit(solution)/shard_map/while/body/eval_jaxpr/qhe,khe->hqk/dot_general | solution.py:80
  393.5 16.0 %multiply_convert_fusion.3 = bf16[4,1024,1024]{1,2,0:T(8,128)(2,1)} fusion(f32[4,1024,1024]{1,2,0:T(8,128)} %get-tuple-element.360, f32[4,1024,1024]{1,2,0:T(8,128)} %fusion.218, f32[4,1024]{1,0:T(4,128)S(1)} %get-tuple-element.361), kind=kLoop, calls=%fused_computation.24.clone.1 | loop fusion | flops 12582912 | bytes 41959424 | tf_op jit(solution)/shard_map/while/body/eval_jaxpr/convert_element_type | solution.py:89
  437.7 13.3 %multiply_reduce_fusion.8 = (f32[4,1024]{1,0:T(4,128)S(1)}, f32[4,1024,1024]{1,2,0:T(8,128)}) fusion(f32[4,1024,1024]{1,2,0:T(8,128)} %fusion.218, f32[4,1024]{1,0:T(4,128)S(1)} %dynamic-slice_bitcast_fusion.2, bf16[3,1024,4,64]{1,3,2,0:T(8,128)(2,1)} %get-tuple-element.407, s32[]{:T(128)S(6)} %copy.89, ...), kind=kOutput, calls=%fused_computation.25.clone.1 | convolution fusion | flops 557838336 | bytes 35685376 | tf_op jit(solution)/shard_map/while/body/eval_jaxpr/qhe,khe->hqk/dot_general | solution.py:80
  451.1 15.7 %multiply_convert_fusion.3 = bf16[4,1024,1024]{1,2,0:T(8,128)(2,1)} fusion(f32[4,1024,1024]{1,2,0:T(8,128)} %get-tuple-element.360, f32[4,1024,1024]{1,2,0:T(8,128)} %fusion.218, f32[4,1024]{1,0:T(4,128)S(1)} %get-tuple-element.361), kind=kLoop, calls=%fused_computation.24.clone.1 | loop fusion | flops 12582912 | bytes 41959424 | tf_op jit(solution)/shard_map/while/body/eval_jaxpr/convert_element_type | solution.py:89
  495.4 13.1 %multiply_reduce_fusion.8 = (f32[4,1024]{1,0:T(4,128)S(1)}, f32[4,1024,1024]{1,2,0:T(8,128)}) fusion(f32[4,1024,1024]{1,2,0:T(8,128)} %fusion.218, f32[4,1024]{1,0:T(4,128)S(1)} %dynamic-slice_bitcast_fusion.2, bf16[3,1024,4,64]{1,3,2,0:T(8,128)(2,1)} %get-tuple-element.407, s32[]{:T(128)S(6)} %copy.89, ...), kind=kOutput, calls=%fused_computation.25.clone.1 | convolution fusion | flops 557838336 | bytes 35685376 | tf_op jit(solution)/shard_map/while/body/eval_jaxpr/qhe,khe->hqk/dot_general | solution.py:80
  508.6 15.9 %multiply_convert_fusion.3 = bf16[4,1024,1024]{1,2,0:T(8,128)(2,1)} fusion(f32[4,1024,1024]{1,2,0:T(8,128)} %get-tuple-element.360, f32[4,1024,1024]{1,2,0:T(8,128)} %fusion.218, f32[4,1024]{1,0:T(4,128)S(1)} %get-tuple-element.361), kind=kLoop, calls=%fused_computation.24.clone.1 | loop fusion | flops 12582912 | bytes 41959424 | tf_op jit(solution)/shard_map/while/body/eval_jaxpr/convert_element_type | solution.py:89
  579.9 18.1 %add_convert_fusion = bf16[3072,1024]{1,0:T(8,128)(2,1)} fusion(f32[3072,1024]{1,0:T(8,128)} %get-tuple-element.230, f32[3072,1024]{1,0:T(8,128)} %reduce-scatter.9.cloned.1.call-done, f32[3072,1024]{1,0:T(8,128)} %get-tuple-element.256, bf16[3072,128]{0,1:T(8,128)(2,1)S(1)} %copy-done.50, bf16[4096,128]{1,0:T(8,128)(2,1)} %param.37, s32[]{:T(128)S(6)} %select_n.15), kind=kOutput, calls=%fused_computation.66 | convolution fusion | flops 852492288 | bytes 45088772 | tf_op jit(solution)/shard_map/dot_general | solution.py:28
  597.9 12.4 %fusion.137 = f32[3072,1024]{1,0:T(8,128)} fusion(bf16[3072,1024]{1,0:T(8,128)(2,1)} %add_convert_fusion, bf16[1024,1024]{1,0:T(8,128)(2,1)S(1)} %copy-done.46), kind=kOutput, calls=%fused_computation.214 | convolution fusion | flops 6442450944 | bytes 20971520 | tf_op jit(solution)/shard_map/dot_general | solution.py:28
  644.4 118.0 %all-gather.8.cloned.1.call-done = bf16[3072,4096]{1,0:T(8,128)(2,1)} async-done(((bf16[3072,1024]{1,0:T(8,128)(2,1)}), bf16[3072,4096]{1,0:T(8,128)(2,1)}) %all-gather.8.cloned.1.call-update) | async-done | bytes 25165840 | tf_op jit(solution)/shard_map/all_gather | solution.py:197
  762.4 12.3 %convolution_convert_fusion.3 = bf16[3072,128]{1,0:T(8,128)(2,1)S(1)} fusion(bf16[3072,4096]{1,0:T(8,128)(2,1)} %all-gather.8.cloned.1.call-done, bf16[4096,128]{1,0:T(8,128)(2,1)S(1)} %copy-done.49), kind=kOutput, calls=%fused_computation.109 | convolution fusion | flops 3221618688 | bytes 27000832 | tf_op jit(solution)/shard_map/dot_general | solution.py:18
  784.1 105.5 %all-reduce.11 = (bf16[3072,128]{1,0:T(8,128)(2,1)S(1)}, bf16[3072,128]{1,0:T(8,128)(2,1)}) all-reduce(f32[3072,128]{1,0:T(8,128)} %convolution_multiply_fusion.6, f32[3072,128]{1,0:T(8,128)} %convolution_multiply_fusion.7), channel_id=1, replica_groups=mesh['dp'=8,'mp'=4] {'mp'}, use_global_device_ids=true, to_apply=%region_20.21 | all-reduce | flops 786432 | bytes 4718592 | tf_op jit(solution)/shard_map/psum | solution.py:252
  901.7 12.0 fusion.133
  922.0 89.1 %reduce-scatter.11.cloned.1.call-done = f32[3072,256]{1,0:T(8,128)} async-done(((f32[3072,1024]{1,0:T(8,128)}), f32[3072,256]{1,0:T(8,128)}) %reduce-scatter.11.cloned.1.call-update) | async-done | bytes 3145744 | tf_op jit(solution)/shard_map/reduce_scatter | solution.py:278
  1028.6 42.5 %all-reduce = (f32[1024]{0:T(1024)}, f32[1024]{0:T(1024)}, f32[1024]{0:T(1024)}, f32[1024]{0:T(1024)}) all-reduce(f32[1024]{0:T(1024)S(1)} %dynamic_update_slice.54, f32[1024]{0:T(1024)S(1)} %dynamic_update_slice.55, f32[1024]{0:T(1024)S(1)} %dynamic_update_slice.56, ...), channel_id=1, replica_groups=mesh['dp'=8,'mp'=4] {'dp','mp'}, use_global_device_ids=true, to_apply=%region_26.27 | all-reduce | flops 4096 | bytes 32768 | tf_op jit(solution)/shard_map/psum | solution.py:351
  1079.3 123.1 %all-reduce.9.cloned.1.call-done = (f32[1024,128]{1,0:T(8,128)}, f32[128,3072]{1,0:T(8,128)}, f32[1024,128]{1,0:T(8,128)}, f32[128,1024]{1,0:T(8,128)}, f32[1024...) async-done(((f32[1024,128]{1,0:T(8,128)}, f32[128,3072]{1,0:T(8,128)}, f32[1024,128]{1,0:T(8,128)}, f32[128,1024]{1,0:T(8,128)}, ...) | async-done | bytes 8388624 | tf_op jit(solution)/shard_map/psum | solution.py:351
  (278 shorter events, 360.6 us)
Async XLA Ops:
  7.2 52.3 %all-gather.4.cloned.1.call-start = ((), (), s32[]{:S(2)}) async-start(), calls=%async_computation.4 | async-start | bytes 7864320 | tf_op jit(solution)/shard_map/all_gather | solution.py:149
  7.9 347.1 %reduce-scatter.5.cloned.1.call-start = ((), (), s32[]{:S(2)}) async-start(), calls=%async_computation.7 | async-start | bytes 15728640 | tf_op jit(solution)/shard_map/reduce_scatter | solution.py:209
  15.9 562.9 %reduce-scatter.9.cloned.1.call-start = ((), (), s32[]{:S(2)}) async-start(), calls=%async_computation.9 | async-start | bytes 62914560 | tf_op jit(solution)/shard_map/reduce_scatter | solution.py:215
  37.7 585.1 %all-gather.6.cloned.1.call-start = ((), (), s32[]{:S(2)}) async-start(), calls=%async_computation.5 | async-start | bytes 7864320 | tf_op jit(solution)/shard_map/all_gather | solution.py:191
  38.3 93.9 %copy-start.28 = (f32[1024,16]{0,1:T(8,128)}, f32[1024,16]{0,1:T(8,128)S(1)}, u32[]{:S(2)}) copy-start(f32[1024,16]{0,1:T(8,128)S(1)} %get-tuple-element.261) | copy-start | bytes 196612
  38.3 93.9 %copy-start.30 = (f32[1024,16]{0,1:T(8,128)}, f32[1024,16]{0,1:T(8,128)S(1)}, u32[]{:S(2)}) copy-start(f32[1024,16]{0,1:T(8,128)S(1)} %get-tuple-element.260) | copy-start | bytes 196612
  66.3 10.9 copy-start.36
  66.3 10.9 copy-start.39
  194.2 11.3 copy-start.18
  194.2 568.2 %all-gather.8.cloned.1.call-start = ((), (), s32[]{:S(2)}) async-start(), calls=%async_computation.6 | async-start | bytes 31457280 | tf_op jit(solution)/shard_map/all_gather | solution.py:197
  237.9 678.4 %reduce-scatter.7.cloned.1.call-start = ((), (), s32[]{:S(2)}) async-start(), calls=%async_computation.8 | async-start | bytes 15728640 | tf_op jit(solution)/shard_map/reduce_scatter | solution.py:272
  355.0 9.9 copy-start.16
  393.5 19.1 %copy-start.1 = (f32[4,1024,1024]{1,2,0:T(8,128)S(1)}, f32[4,1024,1024]{1,2,0:T(8,128)}, u32[]{:S(2)}) copy-start(f32[4,1024,1024]{1,2,0:T(8,128)} %get-tuple-element.360) | copy-start | bytes 50331652 | tf_op jit(solution)/shard_map/while
  451.1 19.1 %copy-start.1 = (f32[4,1024,1024]{1,2,0:T(8,128)S(1)}, f32[4,1024,1024]{1,2,0:T(8,128)}, u32[]{:S(2)}) copy-start(f32[4,1024,1024]{1,2,0:T(8,128)} %get-tuple-element.360) | copy-start | bytes 50331652 | tf_op jit(solution)/shard_map/while
  508.6 19.1 %copy-start.1 = (f32[4,1024,1024]{1,2,0:T(8,128)S(1)}, f32[4,1024,1024]{1,2,0:T(8,128)}, u32[]{:S(2)}) copy-start(f32[4,1024,1024]{1,2,0:T(8,128)} %get-tuple-element.360) | copy-start | bytes 50331652 | tf_op jit(solution)/shard_map/while
  578.8 432.3 %reduce-scatter.11.cloned.1.call-start = ((), (), s32[]{:S(2)}) async-start(), calls=%async_computation.10 | async-start | bytes 15728640 | tf_op jit(solution)/shard_map/reduce_scatter | solution.py:278
  579.9 18.1 %copy-start.46 = (bf16[1024,1024]{1,0:T(8,128)(2,1)S(1)}, bf16[1024,1024]{1,0:T(8,128)(2,1)}, u32[]{:S(2)}) copy-start(bf16[1024,1024]{1,0:T(8,128)(2,1)} %param.29) | copy-start | bytes 6291460
  610.4 592.0 %all-reduce.9.cloned.1.call-start = ((), (), s32[]{:S(2)}) async-start(), calls=%async_computation.11 | async-start | bytes 16777216 | tf_op jit(solution)/shard_map/psum | solution.py:351
  640.6 121.8 %copy-start.49 = (bf16[4096,128]{1,0:T(8,128)(2,1)S(1)}, bf16[4096,128]{1,0:T(8,128)(2,1)}, u32[]{:S(2)}) copy-start(bf16[4096,128]{1,0:T(8,128)(2,1)} %param.37) | copy-start | bytes 3145732
  762.4 13.3 %copy-start.4 = (bf16[3072,256]{1,0:T(8,128)(2,1)S(1)}, bf16[3072,256]{1,0:T(8,128)(2,1)}, u32[]{:S(2)}) copy-start(bf16[3072,256]{1,0:T(8,128)(2,1)} %param.39) | copy-start | bytes 4718596
  891.9 9.7 copy-start.21
  901.6 12.1 copy-start.7
  901.7 12.1 copy-start.15
  1011.1 60.1 %copy-start.37 = (f32[3072]{0:T(1024)S(1)}, f32[3072]{0:T(1024)}, u32[]{:S(2)}) copy-start(f32[3072]{0:T(1024)} %copy-done.36) | copy-start | bytes 36868
  (46 other events, 220.9 us)
Sparse Core Ops, SparseCore 0:
  9.6 49.8 all-gather.3
  62.1 99.0 reduce-scatter.4
  163.8 393.7 reduce-scatter.8
  559.6 46.3 all-gather.5
  607.6 154.8 all-gather.7
  765.0 144.5 reduce-scatter.6
  912.4 98.6 reduce-scatter.10
  1019.8 182.5 all-reduce.8
where the time goes:
time: 1230 us; the launch traced here: 1220 us
  matrix products  368 us (30%)
  waiting for transfers between devices  352 us (29%)
  blocking collectives  269 us (22%)
  local copies, waits for them, and re-layouts  120 us (10%)
  other arithmetic  95.3 us (8%)
  between operations  15.2 us (1%)
    psum x1, waiting for transfers between devices, on_device(): lax.psum((padded[0], padded[1], padded[2], padded[3], padded[4], padded[5...  123 us
    all_gather x1, waiting for transfers between devices, on_device(): lax.all_gather(a, 'mp', axis=1, tiled=True)  118 us
    psum x1, blocking collectives, on_device(): lax.psum((ADAPTER_SCALE * matrix_product_transposed_right(cotangent, outp...  111 us
    psum x1, blocking collectives, on_device(): lax.psum((ADAPTER_SCALE * matrix_product_transposed_right(mixed_gradient,...  105 us
    dot_general x12, matrix products, matrix_product_transposed_right(): lax.dot_general(left, right, (((1,), (1,)), ((), ())), preferred_element_...  102 us
    dot_general x12, matrix products, matrix_product(): return jnp.dot(left, right, preferred_element_type=jnp.float32)  97.3 us
    reduce_scatter x1, waiting for transfers between devices, on_device(): lax.psum_scatter(matrix_product_transposed_right(upper_gradient, expand_f...  89.1 us
    convert_element_type x3, other arithmetic, attend_back(): grad_scores = (probs * (grad_probs - inner)).astype(jnp.bfloat16)  47.5 us
  transfers between devices with their start and end apart: 8, of which 4 were waited for; matrix products, arithmetic and copies ran while one was open for 45% of the time, Pallas kernels for 0%

commit v1 on v0

--- a/solution.py
+++ b/solution.py
@@ -1,8 +1,10 @@
-from functools import partial
+from functools import partial, reduce
 
 import jax
 import jax.numpy as jnp
 from jax import lax
+from jax.experimental import pallas as pl
+from jax.experimental.pallas import tpu as pltpu
 from jax.sharding import PartitionSpec as P
 
 ROTARY = 16
@@ -383,9 +385,835 @@
     )
 
 
+BF = jnp.bfloat16
+F32 = jnp.float32
+BLOCK = 256
+VMEM_LIMIT = 62 << 20
+
+
+def nn(left, right):
+    return lax.dot_general(left, right, (((1,), (0,)), ((), ())), preferred_element_type=F32)
+
+
+def nt(left, right):
+    return lax.dot_general(left, right, (((1,), (1,)), ((), ())), preferred_element_type=F32)
+
+
+def span(start, size, unit=128):
+    return pl.ds(pl.multiple_of(start, unit), size)
+
+
+def quarter_block(pieces, k, j, blocks):
+    if k < 3:
+        return pieces[k], j * BLOCK
+    half = blocks // 2
+    return (pieces[3], j * BLOCK) if j < half else (pieces[4], (j - half) * BLOCK)
+
+
+def layer_norm(rows_f32):
+    center = rows_f32 - jnp.mean(rows_f32, 1, keepdims=True)
+    factor = lax.rsqrt(jnp.mean(center * center, 1, keepdims=True) + EPS)
+    return center * factor, factor
+
+
+def attention_kernel(slot, shared, n_w, ids, *refs):
+    h_refs, g_refs = refs[0:4], refs[4:8]
+    w_refs = refs[8 : 8 + n_w]
+    o_own, o_mate = refs[8 + n_w : 10 + n_w]
+    o_foreign, o_diag = refs[10 + n_w : 15 + n_w], refs[15 + n_w : 20 + n_w]
+    rest = refs[20 + n_w :]
+    gain, bias, up, ja, oa, ou, cos_ref, sin_ref = rest[:8]
+    rest = rest[8:]
+    n_out = 4 if shared else 2
+    outs = rest[:n_out]
+    (h_v, g_v, w_v, o_v, w_t, q_t, k_t, v_t, k_n, v_n, do_t, dm_t, ctx_t, dk, dv, both, tok_sem, w_sem) = rest[n_out:]
+    f, q = ids[0], ids[1]
+    seq = h_v.shape[0]
+    steps = seq // BLOCK
+    heads = q_t.shape[0] // HEAD_DIM
+    width = h_v.shape[1]
+    piece = width // 4
+    for t in range(steps):
+        rows = slice(t * BLOCK, (t + 1) * BLOCK)
+        for s in range(4):
+            cols = slice(s * piece, (s + 1) * piece)
+            pltpu.make_async_copy(h_refs[s].at[rows, :], h_v.at[rows, cols], tok_sem.at[0, t]).start()
+            pltpu.make_async_copy(g_refs[s].at[rows, :], g_v.at[rows, cols], tok_sem.at[1, t]).start()
+    if n_w == 1:
+        for s in range(4):
+            pltpu.make_async_copy(
+                w_refs[0].at[span(lax.bitwise_xor(f, s) * piece, piece), :],
+                w_v.at[s * piece : (s + 1) * piece, :],
+                w_sem.at[0],
+            ).start()
+    else:
+        for k in range(4):
+            row = lax.bitwise_xor(lax.bitwise_xor(q, k), f) * piece
+            for j in range(3):
+                ref, at = quarter_block(w_refs, k, j, 4)
+                pltpu.make_async_copy(
+                    ref.at[at : at + BLOCK, :],
+                    w_v.at[span(row, piece), j * BLOCK : (j + 1) * BLOCK],
+                    w_sem.at[0],
+                ).start()
+    head_block = lax.bitwise_xor(f, slot)
+    for s, ref in ((0, o_own), (1, o_mate)):
+        pltpu.make_async_copy(
+            ref.at[span(head_block * BLOCK, BLOCK), :], o_v.at[:, s * piece : (s + 1) * piece], w_sem.at[1]
+        ).start()
+    for s, pieces in ((2, o_foreign), (3, o_diag)):
+        for k in range(4):
+            ref, at = quarter_block(pieces, k, 3, 4)
+
+            @pl.when(lax.bitwise_xor(q, k) == head_block)
+            def _():
+                pltpu.make_async_copy(
+                    ref.at[at : at + BLOCK, :], o_v.at[:, s * piece : (s + 1) * piece], w_sem.at[1]
+                ).start()
+
+    pltpu.make_async_copy(w_v, w_v, w_sem.at[0]).wait()
+    pltpu.make_async_copy(o_v, o_v, w_sem.at[1]).wait()
+    w_t[...] = w_v[...].T
+    up_t = up[...].T
+    o_rows = o_v[...]
+
+    def project(t):
+        rows = slice(t * BLOCK, (t + 1) * BLOCK)
+        pltpu.make_async_copy(h_v.at[rows, :], h_v.at[rows, :], tok_sem.at[0, t]).wait()
+        pltpu.make_async_copy(g_v.at[rows, :], g_v.at[rows, :], tok_sem.at[1, t]).wait()
+        unit, _ = layer_norm(h_v[rows, :].astype(F32))
+        n = (unit * gain[...] + bias[...]).astype(BF)
+        low = (nn(n, ja[...]).astype(BF) * ADAPTER_SCALE).astype(BF)
+        mixed = nt(w_t[...], n) + nt(up_t, low)
+        cos, sin = cos_ref[:, rows], sin_ref[:, rows]
+        half = ROTARY // 2
+        for h in range(heads):
+            own = slice(h * HEAD_DIM, (h + 1) * HEAD_DIM)
+            base = 3 * HEAD_DIM * h
+            for part in range(2):
+                block = mixed[base + part * HEAD_DIM : base + (part + 1) * HEAD_DIM]
+                a, b = block[:half], block[half:ROTARY]
+                block = jnp.concatenate([a * cos - b * sin, b * cos + a * sin, block[ROTARY:]], 0).astype(BF)
+                if part == 0:
+                    q_t[own, rows] = (block * HEAD_DIM ** (-0.5)).astype(BF)
+                else:
+                    k_t[own, rows] = block
+                    k_n[rows, own] = block.T
+            block = mixed[base + 2 * HEAD_DIM : base + 3 * HEAD_DIM].astype(BF)
+            v_t[own, rows] = block
+            v_n[rows, own] = block.T
+        g = g_v[rows, :]
+        low_grad = (nt(g, ou[...]) * ADAPTER_SCALE).astype(BF)
+        do_t[:, rows] = (nt(o_rows, g) + nt(oa[...], low_grad)).astype(BF)
+
+    for t in range(steps):
+        project(t)
+
+    later = lax.broadcasted_iota(jnp.int32, (BLOCK, BLOCK), 0) > lax.broadcasted_iota(jnp.int32, (BLOCK, BLOCK), 1)
+    state = {}
+
+    def products(h, i):
+        own, qs = slice(h * HEAD_DIM, (h + 1) * HEAD_DIM), slice(i * BLOCK, (i + 1) * BLOCK)
+        state[h, i] = (
+            [nn(k_n[j * BLOCK : (j + 1) * BLOCK, own], q_t[own, qs]) for j in range(i + 1)],
+            [nn(v_n[j * BLOCK : (j + 1) * BLOCK, own], do_t[own, qs]) for j in range(i + 1)],
+        )
+
+    def soft(h, i):
+        scores, d_probs = state[h, i]
+        scores[-1] = jnp.where(later, -1e30, scores[-1])
+        peak = reduce(jnp.maximum, [jnp.max(s, 0, keepdims=True) for s in scores])
+        weights = [jnp.exp(s - peak) for s in scores]
+        inverse = 1.0 / reduce(jnp.add, [jnp.sum(w, 0, keepdims=True) for w in weights])
+        probs = [w * inverse for w in weights]
+        inner = reduce(jnp.add, [jnp.sum(p * d, 0, keepdims=True) for p, d in zip(probs, d_probs)])
+        state[h, i] = (
+            [p.astype(BF) for p in probs],
+            [(p * (d - inner)).astype(BF) for p, d in zip(probs, d_probs)],
+        )
+
+    def unturn(block, cos, sin):
+        half = ROTARY // 2
+        a, b = block[:half], block[half:ROTARY]
+        return jnp.concatenate([a * cos + b * sin, b * cos - a * sin, block[ROTARY:]], 0).astype(BF)
+
+    def finish_block(h, i):
+        own, qs = slice(h * HEAD_DIM, (h + 1) * HEAD_DIM), slice(i * BLOCK, (i + 1) * BLOCK)
+        base = 3 * HEAD_DIM * h
+        probs, d_scores = state.pop((h, i))
+        keys = slice(0, (i + 1) * BLOCK)
+        ctx_t[own, qs] = nn(v_t[own, keys], jnp.concatenate(probs, 0)).astype(BF)
+        d_query = nn(k_t[own, keys], jnp.concatenate(d_scores, 0)) * HEAD_DIM ** (-0.5)
+        dm_t[base : base + HEAD_DIM, qs] = unturn(d_query, cos_ref[:, qs], sin_ref[:, qs])
+        query, d_out = q_t[own, qs], do_t[own, qs]
+        for j in range(i + 1):
+            js = slice(j * BLOCK, (j + 1) * BLOCK)
+            if j == i:
+                dk[own, js] = nt(query, d_scores[j])
+                dv[own, js] = nt(d_out, probs[j])
+            else:
+                dk[own, js] += nt(query, d_scores[j])
+                dv[own, js] += nt(d_out, probs[j])
+        if i == steps - 1:
+            dm_t[base + HEAD_DIM : base + 2 * HEAD_DIM, :] = unturn(dk[own, :], cos_ref[...], sin_ref[...])
+            dm_t[base + 2 * HEAD_DIM : base + 3 * HEAD_DIM, :] = dv[own, :].astype(BF)
+
+    order = [(h, i) for h in range(heads) for i in range(steps)]
+    for at in range(len(order) + 2):
+        if at < len(order):
+            products(*order[at])
+        if at >= 2:
+            finish_block(*order[at - 2])
+        if 1 <= at <= len(order):
+            soft(*order[at - 1])
+    both[:, :BLOCK] = ctx_t[...].T
+    both[:, BLOCK:] = dm_t[...].T
+    if shared:
+        for s in range(4):
+            outs[s][...] = both[span(lax.bitwise_xor(f, s) * BLOCK, BLOCK), :]
+    else:
+        c = lax.bitwise_and(f, 1)
+        half = seq // 2
+        outs[0][...] = both[span(c * half, half), :]
+        outs[1][...] = both[span((1 - c) * half, half), :]
+
+
+def any_spec():
+    return pl.BlockSpec(memory_space=pl.ANY)
+
+
+def vmem_spec():
+    return pl.BlockSpec(memory_space=pltpu.VMEM)
+
+
+def smem_spec():
+    return pl.BlockSpec(memory_space=pltpu.SMEM)
+
+
+def attention(slot, shared, ids, hs, gs, ws, os, gain, bias, up, ja, oa, ou, cos, sin):
+    seq, piece = hs[0].shape
+    width = 4 * piece
+    shard = up.shape[1] // 4
+    heads = shard // (3 * HEAD_DIM)
+    inner = heads * HEAD_DIM
+    rank = ja.shape[1]
+    n_w = len(ws)
+    if shared:
+        out_shape = [jax.ShapeDtypeStruct((BLOCK, inner + shard), BF)] * 4
+    else:
+        out_shape = [jax.ShapeDtypeStruct((seq // 2, inner + shard), BF)] * 2
+    return pl.pallas_call(
+        partial(attention_kernel, slot, shared, n_w),
+        in_specs=[smem_spec()] + [any_spec()] * (8 + n_w + 12) + [vmem_spec()] * 8,
+        out_specs=[vmem_spec()] * len(out_shape),
+        out_shape=out_shape,
+        scratch_shapes=[
+            pltpu.VMEM((seq, width), BF),
+            pltpu.VMEM((seq, width), BF),
+            pltpu.VMEM((width, shard), BF),
+            pltpu.VMEM((inner, width), BF),
+            pltpu.VMEM((shard, width), BF),
+            pltpu.VMEM((inner, seq), BF),
+            pltpu.VMEM((inner, seq), BF),
+            pltpu.VMEM((inner, seq), BF),
+            pltpu.VMEM((seq, inner), BF),
+            pltpu.VMEM((seq, inner), BF),
+            pltpu.VMEM((inner, seq), BF),
+            pltpu.VMEM((shard, seq), BF),
+            pltpu.VMEM((inner, seq), BF),
+            pltpu.VMEM((inner, seq), F32),
+            pltpu.VMEM((inner, seq), F32),
+            pltpu.VMEM((seq, inner + shard), BF),
+            pltpu.SemaphoreType.DMA((2, seq // BLOCK)),
+            pltpu.SemaphoreType.DMA((2,)),
+        ],
+        compiler_params=pltpu.CompilerParams(vmem_limit_bytes=VMEM_LIMIT),
+        cost_estimate=pl.CostEstimate(flops=22_000_000_000, bytes_accessed=12_000_000, transcendentals=3_000_000),
+        name="attention",
+    )(
+        ids, *hs, *gs, *ws, *os, gain, bias,
+        lax.slice_in_dim(up, slot * shard, (slot + 1) * shard, axis=1),
+        ja,
+        lax.slice_in_dim(oa, slot * inner, (slot + 1) * inner, axis=0),
+        ou, cos, sin,
+    )
+
+
+def token_copies(ids, own_refs, shared_refs, dst, sem):
+    f = ids[0]
+    c = lax.bitwise_and(f, 1)
+    half = own_refs[0].shape[0] // 2
+    piece = own_refs[0].shape[1]
+    for s in range(4):
+        cols = slice(s * piece, (s + 1) * piece)
+        pltpu.make_async_copy(own_refs[s].at[span(c * half, half), :], dst.at[:half, cols], sem).start()
+        pltpu.make_async_copy(
+            shared_refs[s].at[span(f * BLOCK, BLOCK), :], dst.at[half : half + BLOCK, cols], sem
+        ).start()
+
+
+def arrived(dst, sem):
+    pltpu.make_async_copy(dst, dst, sem).wait()
+
+
+def finish_kernel(ids, *refs):
+    h_own, h_sh, g_own, g_sh = refs[0:4], refs[4:8], refs[8:12], refs[12:16]
+    a_own, a_sh = refs[16:20], refs[20:24]
+    w_own, w_mate, o_own, o_mate = refs[24:28]
+    p_foreign, p_diag = refs[28:33], refs[33:38]
+    gain, bias, up, ja, oa, ou = refs[38:44]
+    attn, e_one, grads, sums = refs[44:48]
+    h_v, g_v, c_v, m_v, w_v, o_v, sem = refs[48:]
+    f, q = ids[0], ids[1]
+    rows, width = h_v.shape
+    piece = width // 4
+    half = rows - BLOCK
+    shard = m_v.shape[1] // 4
+    token_copies(ids, h_own, h_sh, h_v, sem.at[0])
+    token_copies(ids, g_own, g_sh, g_v, sem.at[1])
+    for s in range(4):
+        for src, dst in ((a_own[s], slice(0, half)), (a_sh[s], slice(half, rows))):
+            pltpu.make_async_copy(src.at[:, :BLOCK], c_v.at[dst, s * BLOCK : (s + 1) * BLOCK], sem.at[2]).start()
+            pltpu.make_async_copy(src.at[:, BLOCK:], m_v.at[dst, s * shard : (s + 1) * shard], sem.at[3]).start()
+    for s, o_ref, w_ref in ((0, o_own, w_own), (1, o_mate, w_mate)):
+        for t in range(4):
+            src, dst = span(lax.bitwise_xor(f, t) * piece, piece), slice(t * piece, (t + 1) * piece)
+            pltpu.make_async_copy(o_ref.at[src, :], o_v.at[dst, s * piece : (s + 1) * piece], sem.at[4]).start()
+            pltpu.make_async_copy(w_ref.at[src, :], w_v.at[dst, s * shard : (s + 1) * shard], sem.at[5]).start()
+    for s, pieces in ((2, p_foreign), (3, p_diag)):
+        for k in range(4):
+            dst = span(lax.bitwise_xor(lax.bitwise_xor(q, k), f) * piece, piece)
+            ref, at = quarter_block(pieces, k, 3, 4)
+            pltpu.make_async_copy(
+                ref.at[at : at + BLOCK, :], o_v.at[dst, s * piece : (s + 1) * piece], sem.at[4]
+            ).start()
+            for j in range(3):
+                ref, at = quarter_block(pieces, k, j, 4)
+                pltpu.make_async_copy(
+                    ref.at[at : at + BLOCK, :],
+                    w_v.at[dst, s * shard + j * BLOCK : s * shard + (j + 1) * BLOCK],
+                    sem.at[5],
+                ).start()
+    for i, dst in ((0, h_v), (1, g_v), (2, c_v), (4, o_v)):
+        arrived(dst, sem.at[i])
+    g = g_v[...]
+    ctx = c_v[...]
+    low_out = nn(ctx, oa[...]).astype(BF)
+    low_out = (low_out * ADAPTER_SCALE).astype(BF)
+    for t in range(rows // BLOCK):
+        ts = slice(t * BLOCK, (t + 1) * BLOCK)
+        attn[ts, :] = nn(c_v[ts, :], o_v[...]) + nn(low_out[ts], ou[...])
+    low_out_grad = (nt(g, ou[...]) * ADAPTER_SCALE).astype(BF)
+
+    def put(base, size, value):
+        for s in range(4):
+            grads[:, span(base + lax.bitwise_xor(f, s) * size, size)] = value[:, s * size : (s + 1) * size]
+
+    put(0, piece, nn(low_out.T, g))
+    put(width, piece, nn(low_out_grad.T, ctx))
+    arrived(m_v, sem.at[3])
+    arrived(w_v, sem.at[5])
+    unit, _ = layer_norm(h_v[...].astype(F32))
+    n = (unit * gain[...] + bias[...]).astype(BF)
+    low = (nn(n, ja[...]).astype(BF) * ADAPTER_SCALE).astype(BF)
+    low_grad = (nt(m_v[...], up[...]) * ADAPTER_SCALE).astype(BF)
+    put(2 * width, shard, nn(low.T, m_v[...]))
+    put(2 * width + 4 * shard, piece, nn(low_grad.T, n))
+    total = [None, None]
+    for t in range(rows // BLOCK):
+        ts = slice(t * BLOCK, (t + 1) * BLOCK)
+        d_norm = nt(m_v[ts, :], w_v[...]) + nt(low_grad[ts], ja[...])
+        part = (jnp.sum(d_norm * unit[ts], 0, keepdims=True), jnp.sum(d_norm, 0, keepdims=True))
+        total = [p if o is None else o + p for o, p in zip(total, part)]
+        e_one[ts, :] = d_norm * gain[...]
+    put_sums(sums, f, total)
+
+
+def put_sums(sums, f, total):
+    piece = sums.shape[1] // 4
+    value = jnp.concatenate(list(total) + [jnp.zeros((6, sums.shape[1]), F32)], 0)
+    for s in range(4):
+        sums[:, span(lax.bitwise_xor(f, s) * piece, piece)] = value[:, s * piece : (s + 1) * piece]
+
+
+def finish_tokens(ids, hs, hsh, gs, gsh, a_own, a_sh, weights, gain, bias, up, ja, oa, ou):
+    seq, piece = hs[0].shape
+    width = 4 * piece
+    rows = seq // 2 + BLOCK
+    shard = up.shape[1] // 4
+    rank = ja.shape[1]
+    return pl.pallas_call(
+        finish_kernel,
+        in_specs=[smem_spec()] + [any_spec()] * 38 + [vmem_spec()] * 6,
+        out_specs=[vmem_spec()] * 4,
+        out_shape=[
+            jax.ShapeDtypeStruct((rows, width), F32),
+            jax.ShapeDtypeStruct((rows, width), F32),
+            jax.ShapeDtypeStruct((rank, 3 * width + 4 * shard), F32),
+            jax.ShapeDtypeStruct((8, width), F32),
+        ],
+        scratch_shapes=[
+            pltpu.VMEM((rows, width), BF),
+            pltpu.VMEM((rows, width), BF),
+            pltpu.VMEM((rows, width), BF),
+            pltpu.VMEM((rows, 4 * shard), BF),
+            pltpu.VMEM((width, 4 * shard), BF),
+            pltpu.VMEM((width, width), BF),
+            pltpu.SemaphoreType.DMA((6,)),
+        ],
+        compiler_params=pltpu.CompilerParams(vmem_limit_bytes=VMEM_LIMIT),
+        cost_estimate=pl.CostEstimate(flops=18_000_000_000, bytes_accessed=30_000_000, transcendentals=1000),
+        name="finish_attention",
+    )(ids, *hs, *hsh, *gs, *gsh, *a_own, *a_sh, *weights, gain, bias, up, ja, oa, ou)
+
+
+def load_mlp_weights(ids, e_own, e_mate, s_own, s_mate, p_foreign, p_diag, e_v, s_v, e_sem, s_sem, chunk):
+    f, q = ids[0], ids[1]
+    width, hidden = e_v.shape
+    piece, part = width // 4, hidden // 4
+    per = part // chunk
+    for s, e_ref, s_ref in ((0, e_own, s_own), (1, e_mate, s_mate)):
+        for u in range(per):
+            for t in range(4):
+                pltpu.make_async_copy(
+                    e_ref.at[span(lax.bitwise_xor(f, t) * piece, piece), u * chunk : (u + 1) * chunk],
+                    e_v.at[t * piece : (t + 1) * piece, s * part + u * chunk : s * part + (u + 1) * chunk],
+                    e_sem.at[s * per + u],
+                ).start()
+        for t in range(4):
+            for u in range(per):
+                pltpu.make_async_copy(
+                    s_ref.at[span(lax.bitwise_xor(f, t) * part + u * chunk, chunk), :],
+                    s_v.at[t * part + u * chunk : t * part + (u + 1) * chunk, s * piece : (s + 1) * piece],
+                    s_sem.at[t * per + u],
+                ).start()
+    blocks = 2 * part // BLOCK
+    for s, pieces in ((2, p_foreign), (3, p_diag)):
+        for k in range(4):
+            place = lax.bitwise_xor(lax.bitwise_xor(q, k), f)
+            for j in range(part // BLOCK):
+                ref, at = quarter_block(pieces, k, j, blocks)
+                pltpu.make_async_copy(
+                    ref.at[at : at + BLOCK, :],
+                    e_v.at[span(place * piece, piece), s * part + j * BLOCK : s * part + (j + 1) * BLOCK],
+                    e_sem.at[s * per + j * BLOCK // chunk],
+                ).start()
+            for u in range(per):
+                ref, at = quarter_block(pieces, k, part // BLOCK + u * chunk // BLOCK, blocks)
+                pltpu.make_async_copy(
+                    ref.at[at : at + chunk, :],
+                    s_v.at[span(place * part + u * chunk, chunk), s * piece : (s + 1) * piece],
+                    s_sem.at[place * per + u],
+                ).start()
+
+
+CHUNK = 512
+
+
+def mlp_first_kernel(ids, *refs):
+    h_own, h_sh, g_own, g_sh = refs[0:4], refs[4:8], refs[8:12], refs[12:16]
+    weights = refs[16:30]
+    gain, bias, ea, eu, sa, su = refs[30:36]
+    act_out, dup_out, ls_out, dle_out, grads = refs[36:41]
+    h_v, g_v, n_v, e_v, s_v, act, dup, sem, e_sem, s_sem, o_sem = refs[41:]
+    f = ids[0]
+    rows, width = h_v.shape
+    hidden = e_v.shape[1]
+    token_copies(ids, h_own, h_sh, h_v, sem.at[0])
+    token_copies(ids, g_own, g_sh, g_v, sem.at[1])
+    load_mlp_weights(
+        ids, weights[0], weights[1], weights[2], weights[3], weights[4:9], weights[9:14], e_v, s_v, e_sem, s_sem, CHUNK
+    )
+    arrived(h_v, sem.at[0])
+    unit, _ = layer_norm(h_v[...].astype(F32))
+    n_v[...] = (unit * gain[...] + bias[...]).astype(BF)
+    low = (nn(n_v[...], ea[...]).astype(BF) * ADAPTER_SCALE).astype(BF)
+    arrived(g_v, sem.at[1])
+    low_grad = (nt(g_v[...], su[...]) * ADAPTER_SCALE).astype(BF)
+    state = {}
+
+    def products(b, t):
+        ts, bs = slice(t * BLOCK, (t + 1) * BLOCK), slice(b * CHUNK, (b + 1) * CHUNK)
+        if t == 0:
+            arrived(e_v.at[:, bs], e_sem.at[b])
+            arrived(s_v.at[bs, :], s_sem.at[b])
+        state[b, t] = (
+            nn(n_v[ts, :], e_v[:, bs]) + nn(low[ts], eu[:, bs]),
+            nt(g_v[ts, :], s_v[bs, :]) + nt(low_grad[ts], sa[bs, :]),
+        )
+
+    def bend(b, t):
+        ts, bs = slice(t * BLOCK, (t + 1) * BLOCK), slice(b * CHUNK, (b + 1) * CHUNK)
+        upper, d_active = state.pop((b, t))
+        normal = 0.5 * (1.0 + lax.erf(upper * 0.7071067811865476))
+        density = jnp.exp(-0.5 * upper * upper) * 0.3989422804014327
+        act[ts, bs] = (upper * normal).astype(BF)
+        dup[ts, bs] = (d_active * (normal + upper * density)).astype(BF)
+        if t == rows // BLOCK - 1:
+            pltpu.make_async_copy(act.at[:, bs], act_out.at[:, bs], o_sem.at[0]).start()
+            pltpu.make_async_copy(dup.at[:, bs], dup_out.at[:, bs], o_sem.at[1]).start()
+
+    order = [(b, t) for b in range(hidden // CHUNK) for t in range(rows // BLOCK)]
+    for at in range(len(order) + 1):
+        if at < len(order):
+            products(*order[at])
+        if at > 0:
+            bend(*order[at - 1])
+
+    part, piece = hidden // 4, width // 4
+
+    def put(base, size, value):
+        for s in range(4):
+            grads[:, span(base + lax.bitwise_xor(f, s) * size, size)] = value[:, s * size : (s + 1) * size]
+
+    put(0, part, nn(low_grad.T, act[...]))
+    put(hidden, part, nn(low.T, dup[...]))
+    low_shrink = (nn(act[...], sa[...]).astype(BF) * ADAPTER_SCALE).astype(BF)
+    low_expand_grad = (nt(dup[...], eu[...]) * ADAPTER_SCALE).astype(BF)
+    ls_out[...] = low_shrink
+    dle_out[...] = low_expand_grad
+    put(2 * hidden, piece, nn(low_shrink.T, g_v[...]))
+    put(2 * hidden + width, piece, nn(low_expand_grad.T, n_v[...]))
+    arrived(act, o_sem.at[0])
+    arrived(dup, o_sem.at[1])
+
+
+def mlp_first(ids, hs, hsh, gs, gsh, weights, gain, bias, ea, eu, sa, su):
+    seq, piece = hs[0].shape
+    width = 4 * piece
+    rows = seq // 2 + BLOCK
+    hidden = eu.shape[1]
+    rank = ea.shape[1]
+    return pl.pallas_call(
+        mlp_first_kernel,
+        in_specs=[smem_spec()] + [any_spec()] * 30 + [vmem_spec()] * 6,
+        out_specs=[any_spec()] * 2 + [vmem_spec()] * 3,
+        out_shape=[
+            jax.ShapeDtypeStruct((rows, hidden), BF),
+            jax.ShapeDtypeStruct((rows, hidden), BF),
+            jax.ShapeDtypeStruct((rows, rank), BF),
+            jax.ShapeDtypeStruct((rows, rank), BF),
+            jax.ShapeDtypeStruct((rank, 2 * hidden + 2 * width), F32),
+        ],
+        scratch_shapes=[
+            pltpu.VMEM((rows, width), BF),
+            pltpu.VMEM((rows, width), BF),
+            pltpu.VMEM((rows, width), BF),
+            pltpu.VMEM((width, hidden), BF),
+            pltpu.VMEM((hidden, width), BF),
+            pltpu.VMEM((rows, hidden), BF),
+            pltpu.VMEM((rows, hidden), BF),
+            pltpu.SemaphoreType.DMA((2,)),
+            pltpu.SemaphoreType.DMA((hidden // CHUNK,)),
+            pltpu.SemaphoreType.DMA((hidden // CHUNK,)),
+            pltpu.SemaphoreType.DMA((2,)),
+        ],
+        compiler_params=pltpu.CompilerParams(vmem_limit_bytes=VMEM_LIMIT),
+        cost_estimate=pl.CostEstimate(flops=28_000_000_000, bytes_accessed=40_000_000, transcendentals=3_000_000),
+        name="mlp_first",
+    )(ids, *hs, *hsh, *gs, *gsh, *weights, gain, bias, ea, eu, sa, su)
+
+
+def mlp_second_kernel(ids, *refs):
+    h_own, h_sh, g_own, g_sh = refs[0:4], refs[4:8], refs[8:12], refs[12:16]
+    weights = refs[16:30]
+    act_ref, dup_ref, attn_ref, e_ref = refs[30:34]
+    gain, ea, su, ls, dle = refs[34:39]
+    r_outs, g_outs, sums = refs[39:43], refs[43:47], refs[47]
+    h_v, g_v, e_v, s_v, act, dup, attn, e_one, sem, e_sem, s_sem = refs[48:]
+    f = ids[0]
+    rows, width = h_v.shape
+    hidden = e_v.shape[1]
+    piece = width // 4
+    pltpu.make_async_copy(act_ref, act, sem.at[2]).start()
+    load_mlp_weights(
+        ids, weights[0], weights[1], weights[2], weights[3], weights[4:9], weights[9:14], e_v, s_v, e_sem, s_sem, hidden // 4
+    )
+    pltpu.make_async_copy(dup_ref, dup, sem.at[3]).start()
+    token_copies(ids, h_own, h_sh, h_v, sem.at[0])
+    pltpu.make_async_copy(attn_ref, attn, sem.at[4]).start()
+    token_copies(ids, g_own, g_sh, g_v, sem.at[1])
+    pltpu.make_async_copy(e_ref, e_one, sem.at[5]).start()
+    part = hidden // 4
+    arrived(act, sem.at[2])
+    for b in range(4):
+        arrived(s_v.at[b * part : (b + 1) * part, :], s_sem.at[b])
+    arrived(h_v, sem.at[0])
+    arrived(attn, sem.at[4])
+    for t in range(rows // BLOCK):
+        ts = slice(t * BLOCK, (t + 1) * BLOCK)
+        value = nn(act[ts, :], s_v[...]) + nn(ls[ts, :], su[...])
+        value = (h_v[ts, :].astype(F32) + attn[ts, :] + value).astype(BF)
+        for s in range(4):
+            r_outs[s][ts, :] = value[:, s * piece : (s + 1) * piece]
+    arrived(dup, sem.at[3])
+    for b in range(4):
+        arrived(e_v.at[:, b * part : (b + 1) * part], e_sem.at[b])
+    arrived(g_v, sem.at[1])
+    arrived(e_one, sem.at[5])
+    total = [None, None]
+    for t in range(rows // BLOCK):
+        ts = slice(t * BLOCK, (t + 1) * BLOCK)
+        d_norm = nt(dup[ts, :], e_v[...]) + nt(dle[ts, :], ea[...])
+        unit, factor = layer_norm(h_v[ts, :].astype(F32))
+        sums_here = (jnp.sum(d_norm * unit, 0, keepdims=True), jnp.sum(d_norm, 0, keepdims=True))
+        total = [p if o is None else o + p for o, p in zip(total, sums_here)]
+        e = d_norm * gain[...] + e_one[ts, :]
+        plain = jnp.mean(e, 1, keepdims=True)
+        along = jnp.mean(e * unit, 1, keepdims=True)
+        value = g_v[ts, :].astype(F32) + factor * (e - plain - unit * along)
+        for s in range(4):
+            g_outs[s][ts, :] = value[:, s * piece : (s + 1) * piece].astype(g_outs[s].dtype)
+    put_sums(sums, f, total)
+
+
+def mlp_second(ids, hs, hsh, gs, gsh, weights, act, dup, attn, e_one, gain, ea, su, ls, dle):
+    seq, piece = hs[0].shape
+    width = 4 * piece
+    rows = seq // 2 + BLOCK
+    hidden = act.shape[1]
+    return pl.pallas_call(
+        mlp_second_kernel,
+        in_specs=[smem_spec()] + [any_spec()] * 34 + [vmem_spec()] * 5,
+        out_specs=[vmem_spec()] * 9,
+        out_shape=[jax.ShapeDtypeStruct((rows, piece), BF)] * 4
+        + [
+            jax.ShapeDtypeStruct((rows, piece), F32),
+            jax.ShapeDtypeStruct((rows, piece), F32),
+            jax.ShapeDtypeStruct((rows, piece), BF),
+            jax.ShapeDtypeStruct((rows, piece), BF),
+            jax.ShapeDtypeStruct((8, width), F32),
+        ],
+        scratch_shapes=[
+            pltpu.VMEM((rows, width), BF),
+            pltpu.VMEM((rows, width), BF),
+            pltpu.VMEM((width, hidden), BF),
+            pltpu.VMEM((hidden, width), BF),
+            pltpu.VMEM((rows, hidden), BF),
+            pltpu.VMEM((rows, hidden), BF),
+            pltpu.VMEM((rows, width), F32),
+            pltpu.VMEM((rows, width), F32),
+            pltpu.SemaphoreType.DMA((6,)),
+            pltpu.SemaphoreType.DMA((4,)),
+            pltpu.SemaphoreType.DMA((4,)),
+        ],
+        compiler_params=pltpu.CompilerParams(vmem_limit_bytes=VMEM_LIMIT),
+        cost_estimate=pl.CostEstimate(flops=20_000_000_000, bytes_accessed=45_000_000, transcendentals=1000),
+        name="mlp_second",
+    )(ids, *hs, *hsh, *gs, *gsh, *weights, act, dup, attn, e_one, gain, ea, su, ls, dle)
+
+
+def gather_rows_kernel(widen, ids, *refs):
+    parts, out = refs[:4], refs[4]
+    scratch = refs[5:]
+    f = ids[0]
+    sem = scratch[-1]
+    rows = parts[0].shape[0]
+    half = rows - BLOCK
+    seq = 2 * half
+    copies = []
+    for s in range(4):
+        src = parts[s]
+        if src.dtype != out.dtype:
+            scratch[s - 2][...] = src[...].astype(out.dtype)
+            src = scratch[s - 2]
+        at = lax.bitwise_xor(f, s)
+        copies.append(pltpu.make_async_copy(src.at[:half, :], out.at[span(at * half, half), :], sem.at[2 * s]))
+        copies.append(
+            pltpu.make_async_copy(src.at[half:, :], out.at[span(2 * seq + at * BLOCK, BLOCK), :], sem.at[2 * s + 1])
+        )
+        copies[-2].start()
+        copies[-1].start()
+    for copy in copies:
+        copy.wait()
+
+
+def gather_rows(ids, parts, dtype):
+    rows, piece = parts[0].shape
+    narrow = [p for p in parts if p.dtype != dtype]
+    return pl.pallas_call(
+        partial(gather_rows_kernel, dtype),
+        in_specs=[smem_spec()] + [vmem_spec()] * 4,
+        out_specs=any_spec(),
+        out_shape=jax.ShapeDtypeStruct((4 * rows, piece), dtype),
+        scratch_shapes=[pltpu.VMEM((rows, piece), dtype)] * len(narrow) + [pltpu.SemaphoreType.DMA((8,))],
+        compiler_params=pltpu.CompilerParams(vmem_limit_bytes=VMEM_LIMIT),
+        name="gather_rows",
+    )(ids, *parts)
+
+
+def swap(axis, bit):
+    def run(value):
+        size = lax.axis_size(axis)
+        return lax.ppermute(value, axis, [(i, i ^ bit) for i in range(size)])
+
+    return run
+
+
+def after(value, *others):
+    return lax.optimization_barrier((value, *others))[0]
+
+
+def spread(first, to_y, to_z, to_core):
+    half = first.shape[0] // 2
+    by_y = to_y(first)
+    by_z = to_z(first)
+    third = to_y(lax.slice_in_dim(by_z, 0, half, axis=0))
+    fourth = to_z(lax.slice_in_dim(by_y, half, 2 * half, axis=0))
+    pieces = (first, by_y, by_z, third, fourth)
+    return pieces, tuple(to_core(p) for p in pieces)
+
+
+def all_sum(value, bits, swaps, types):
+    for bit, exchange, dtype in zip(bits, swaps, types):
+        half = value.shape[0] // 2
+        keep = lax.dynamic_slice_in_dim(value, bit * half, half, 0)
+        send = lax.dynamic_slice_in_dim(value, (1 - bit) * half, half, 0)
+        value = keep + exchange(send.astype(dtype)).astype(F32)
+    value = value.astype(BF)
+    for bit, exchange in reversed(list(zip(bits, swaps))):
+        other = exchange(value)
+        value = jnp.where(bit == 0, jnp.concatenate([value, other], 0), jnp.concatenate([other, value], 0))
+    return value.astype(F32)
+
+
+def on_device_by_tokens(
+    hidden,
+    first_gain,
+    first_bias,
+    second_gain,
+    second_bias,
+    joined_frozen_weight,
+    output_frozen_weight,
+    expand_frozen_weight,
+    shrink_frozen_weight,
+    joined_a,
+    joined_up_factor,
+    output_a,
+    output_up_factor,
+    expand_a,
+    expand_up_factor,
+    shrink_a,
+    shrink_up_factor,
+    cotangent,
+):
+    f = lax.axis_index("mp")
+    d = lax.axis_index("dp")
+    x, c, q = f // 2, f % 2, d % 4
+    seq = SEQ_LEN
+    width = 4 * hidden.shape[1]
+    hidden_units = 4 * expand_frozen_weight.shape[1]
+    ids = jnp.stack([f, q]).astype(jnp.int32)
+    to_core, to_x, to_diag = swap("mp", 1), swap("mp", 2), swap("mp", 3)
+    to_y, to_z, to_far = swap("dp", 1), swap("dp", 2), swap("dp", 4)
+
+    def rows_of(array, at):
+        return lax.dynamic_slice_in_dim(array, at * seq, seq, 0)
+
+    def quarter(w):
+        size = w.shape[0] // 4
+        return lax.dynamic_slice_in_dim(w, q * size, size, 0)
+
+    def columns(w):
+        return [lax.slice_in_dim(w, i, i + BLOCK, axis=1) for i in range(0, w.shape[1], BLOCK)]
+
+    pack_one = jnp.concatenate(columns(quarter(joined_frozen_weight)) + [quarter(output_frozen_weight)], 0)
+    pack_two = jnp.concatenate(columns(quarter(expand_frozen_weight)) + [quarter(shrink_frozen_weight)], 0)
+
+    def features(array):
+        own, other, shared = rows_of(array, x), rows_of(array, 1 - x), array[2 * seq :]
+        return own, other, shared
+
+    h_own, h_other, h_shared = features(hidden)
+    g_own, g_other, g_shared = features(cotangent)
+    first_one = to_x(pack_one)
+    hx_own = to_x(h_other)
+    gx_own = to_x(after(g_other, first_one))
+    hx_shared = to_x(after(h_shared, hx_own))
+    gx_shared = to_x(after(g_shared, gx_own))
+    first_two = to_x(after(pack_two, hx_shared))
+    hs = (h_own, to_core(h_own), hx_own, to_core(hx_own))
+    gs = (g_own, to_core(g_own), gx_own, to_core(gx_own))
+    hsh = (h_shared, to_core(h_shared), hx_shared, to_core(hx_shared))
+    gsh = (g_shared, to_core(g_shared), gx_shared, to_core(gx_shared))
+    foreign_one, diag_one = spread(first_one, to_y, to_z, to_core)
+    foreign_two, diag_two = spread(first_two, to_y, to_z, to_core)
+    w_mate, o_mate = to_core(joined_frozen_weight), to_core(output_frozen_weight)
+    e_mate, s_mate = to_core(expand_frozen_weight), to_core(shrink_frozen_weight)
+
+    def ordered(array, axis):
+        size = array.shape[axis] // 4
+        return jnp.concatenate(
+            [lax.dynamic_slice_in_dim(array, (f ^ s) * size, size, axis) for s in range(4)], axis
+        )
+
+    gain_one, bias_one, gain_two, bias_two = (
+        ordered(v, 0)[None, :] for v in (first_gain, first_bias, second_gain, second_bias)
+    )
+    ja, oa, ea, sa = (ordered(v, 0) for v in (joined_a, output_a, expand_a, shrink_a))
+    ju, ou, eu, su = (ordered(v, 1) for v in (joined_up_factor, output_up_factor, expand_up_factor, shrink_up_factor))
+    position = jnp.arange(seq, dtype=F32)[None, :]
+    frequency = 10000.0 ** (-(jnp.arange(ROTARY // 2, dtype=F32) * 2.0) / ROTARY)
+    angles = frequency[:, None] * position
+    cos, sin = jnp.cos(angles), jnp.sin(angles)
+
+    o_parts = (output_frozen_weight, o_mate) + foreign_one + diag_one
+    shared_args = (gain_one, bias_one, ju, ja, oa, ou, cos, sin)
+    keep_a, send_a = attention(0, False, ids, hs, gs, (joined_frozen_weight,), o_parts, *shared_args)
+    b_parts = attention(0, True, ids, hsh, gsh, (joined_frozen_weight,), o_parts, *shared_args)
+    keep_c, send_c = attention(2, False, ids, hs, gs, foreign_one, o_parts, *shared_args)
+    a_own = (keep_a, to_core(send_a), keep_c, to_core(send_c))
+    a_shared = (b_parts[0], to_core(b_parts[1]), to_x(b_parts[2]), to_diag(b_parts[3]))
+
+    attn, e_one, grads_one, sums_one = finish_tokens(
+        ids, hs, hsh, gs, gsh, a_own, a_shared,
+        (joined_frozen_weight, w_mate, output_frozen_weight, o_mate) + foreign_one + diag_one,
+        gain_one, bias_one, ju, ja, oa, ou,
+    )
+    mlp_weights = (expand_frozen_weight, e_mate, shrink_frozen_weight, s_mate) + foreign_two + diag_two
+    act, dup, ls, dle, grads_two = mlp_first(
+        ids, hs, hsh, gs, gsh, mlp_weights, gain_two, bias_two, ea, eu, sa, su
+    )
+    outs = mlp_second(
+        ids, hs, hsh, gs, gsh, mlp_weights, act, dup, attn, e_one, gain_two, ea, su, ls, dle
+    )
+    r, g, sums_two = outs[0:4], outs[4:8], outs[8]
+    result = gather_rows(ids, (r[0], to_core(r[1]), to_x(r[2]), to_diag(r[3])), BF)
+    hidden_grad = gather_rows(ids, (g[0], to_core(g[1]), to_x(g[2]), to_diag(g[3])), F32)
+
+    bits = (c, d % 2, (d // 2) % 2, d // 4, x)
+    swaps = (to_core, to_y, to_z, to_far, to_x)
+    types = (F32, BF, BF, BF, F32)
+    grads_one = all_sum(grads_one, bits, swaps, types)
+    grads_two = all_sum(grads_two, bits, swaps, types)
+    sums = lax.psum(jnp.concatenate([sums_one[:2], sums_two[:2]], 0), ("dp", "mp"))
+    shard_total = ju.shape[1]
+
+    def cut(array, at, size):
+        return lax.slice_in_dim(array, at, at + size, axis=1)
+
+    return (
+        result,
+        hidden_grad,
+        sums[0],
+        sums[1],
+        sums[2],
+        sums[3],
+        cut(grads_one, 2 * width + shard_total, width).T,
+        cut(grads_one, 2 * width, shard_total),
+        cut(grads_one, width, width).T,
+        cut(grads_one, 0, width),
+        cut(grads_two, 2 * hidden_units + width, width).T,
+        cut(grads_two, hidden_units, hidden_units),
+        cut(grads_two, 0, hidden_units).T,
+        cut(grads_two, 2 * hidden_units, width),
+    )
+
+
 def solution(mesh):
+    by_tokens = mesh.shape["mp"] == 4 and mesh.shape["dp"] == 8
     return jax.shard_map(
-        on_device,
+        on_device_by_tokens if by_tokens else on_device,
         mesh=mesh,
         in_specs=(
             P("dp", "mp"),

time: 1230 us -> 507 us (0.41)
  matrix products: 368 us -> 0 us
  blocking collectives: 269 us -> 39.4 us
  waiting for transfers between devices: 352 us -> 182 us
  Pallas kernels: 0 us -> 169 us
  local copies, waits for them, and re-layouts: 120 us -> 40.1 us
  other arithmetic: 95.3 us -> 23.3 us
  starting transfers between devices: 0.54 us -> 41.9 us
  between operations: 15.2 us -> 1.59 us
    dot_general x53 -> x0, matrix products: 368 us -> none  [the longest x12 102 us: matrix_product_transposed_right(): lax.dot_general(left, right, (((1,), (1,)), ((), ())), preferred_element_...]
    psum x4 -> x1, blocking collectives: 269 us -> 39.4 us  [on_device_by_tokens(): lax.psum(jnp.concatenate([sums_one[:2], sums_two[:2]], 0), ('dp', 'mp'))]
    ppermute x0 -> x67, waiting for transfers between devices: none -> 182 us  [run(): return lax.ppermute(value, axis, [(i, i ^ bit) for i in range(size)])]
    pallas_call x0 -> x8, Pallas kernels: none -> 169 us  [the longest x3 69.3 us: attention(): pl.pallas_call(partial(attention_kernel, slot, shared, n_w), in_specs=[sm...]
    all_gather x3 -> x0, waiting for transfers between devices: 139 us -> none  [the longest x1 118 us: on_device(): lax.all_gather(a, 'mp', axis=1, tiled=True)]
    psum x1 -> x0, waiting for transfers between devices: 123 us -> none  [on_device(): lax.psum((padded[0], padded[1], padded[2], padded[3], padded[4], padded[5...]
    reduce_scatter x4 -> x0, waiting for transfers between devices: 89.1 us -> none  [the longest x1 89.1 us: on_device(): lax.psum_scatter(matrix_product_transposed_right(upper_gradient, expand_f...]
    convert_element_type x5 -> x4, other arithmetic: 47.5 us -> 4.38 us  [the longest x2 4.29 us: all_sum(): return value.astype(F32)]
  transfers between devices with their start and end apart: 8 -> 67, of which waited for: 4 -> 27; matrix products, arithmetic and copies ran while one was open for 45% -> 10% of each run, Pallas kernels for 0% -> 34%
where the time goes in v1:
time: 507 us; the launch traced here: 498 us
  waiting for transfers between devices  182 us (36%)
  Pallas kernels  169 us (33%)
  starting transfers between devices  41.9 us (8%)
  local copies, waits for them, and re-layouts  40.1 us (8%)
  blocking collectives  39.4 us (8%)
  other arithmetic  23.3 us (5%)
    ppermute x67, waiting for transfers between devices, run(): return lax.ppermute(value, axis, [(i, i ^ bit) for i in range(size)])  182 us
    pallas_call x3, Pallas kernels, attention(): pl.pallas_call(partial(attention_kernel, slot, shared, n_w), in_specs=[sm...  69.3 us
    ppermute x67, starting transfers between devices, run(): return lax.ppermute(value, axis, [(i, i ^ bit) for i in range(size)])  41.9 us
    pallas_call x1, Pallas kernels, mlp_first(): pl.pallas_call(mlp_first_kernel, in_specs=[smem_spec()] + [any_spec()] *...  39.5 us
    psum x1, blocking collectives, on_device_by_tokens(): lax.psum(jnp.concatenate([sums_one[:2], sums_two[:2]], 0), ('dp', 'mp'))  39.4 us
    pallas_call x1, Pallas kernels, mlp_second(): pl.pallas_call(mlp_second_kernel, in_specs=[smem_spec()] + [any_spec()] *...  29.7 us
    pallas_call x1, Pallas kernels, finish_tokens(): pl.pallas_call(finish_kernel, in_specs=[smem_spec()] + [any_spec()] * 38...  25.1 us
    unnamed x96, local copies, waits for them, and re-layouts  17 us
  transfers between devices with their start and end apart: 67, of which 27 were waited for; matrix products, arithmetic and copies ran while one was open for 10% of the time, Pallas kernels for 34%

profile of v1, /device:TPU:0, one launch (start us, length us, event | category | flops | bytes accessed | tf_op | source)
XLA Modules:
  0.0 498.1 jit_solution(2819432436205246391)
XLA Ops:
  11.9 7.8 %collective-permute-done.7.refs_11_.refs_8_.refs_15_.refs_28_ = bf16[1024,256]{1,0:T(8,128)(2,1)} collective-permute-done((bf16[1024,256]{1,0:T(8,128)(2,1)}, bf16[1024,256]{1,0:T(8,128)(2,1)}, u32[]{:S(2)}, u32[]{:S(2)}) %collective-permute-start.7) | collective-permute-done | bytes 524320 | tf_op jit(solution)/shard_map/ppermute | solution.py:1048
  24.1 6.6 %collective-permute-done.1.refs_2_ = bf16[1024,256]{1,0:T(8,128)(2,1)} collective-permute-done((bf16[1024,256]{1,0:T(8,128)(2,1)}, bf16[1024,256]{1,0:T(8,128)(2,1)}, u32[]{:S(2)}, u32[]{:S(2)}) %collective-permute-start.1) | collective-permute-done | bytes 524320 | tf_op jit(solution)/shard_map/ppermute | solution.py:1048
  39.9 5.9 %collective-permute-done.26.refs_12_.refs_9_.refs_16_.refs_29_ = bf16[1024,256]{1,0:T(8,128)(2,1)} collective-permute-done((bf16[1024,256]{1,0:T(8,128)(2,1)}, bf16[1024,256]{1,0:T(8,128)(2,1)}, u32[]{:S(2)}, u32[]{:S(2)}) %collective-permute-start.26) | collective-permute-done | bytes 524320 | tf_op jit(solution)/shard_map/ppermute | solution.py:1048
  51.8 7.2 %collective-permute-done.4.refs_6_.refs_2_ = bf16[1024,256]{1,0:T(8,128)(2,1)S(1)} collective-permute-done((bf16[1024,256]{1,0:T(8,128)(2,1)S(1)}, bf16[1024,256]{1,0:T(8,128)(2,1)S(1)}, u32[]{:S(2)}, u32[]{:S(2)}) %collective-permute-start.4) | collective-permute-done | bytes 524320 | tf_op jit(solution)/shard_map/ppermute | solution.py:1048
  64.2 7.3 %collective-permute-done.11.refs_14_.refs_6_ = bf16[1024,256]{1,0:T(8,128)(2,1)} collective-permute-done((bf16[1024,256]{1,0:T(8,128)(2,1)}, bf16[1024,256]{1,0:T(8,128)(2,1)}, u32[]{:S(2)}, u32[]{:S(2)}) %collective-permute-start.11) | collective-permute-done | bytes 524320 | tf_op jit(solution)/shard_map/ppermute | solution.py:1048
  73.3 23.2 %attention.4 = (bf16[512,1024]{1,0:T(8,128)(2,1)}, bf16[512,1024]{1,0:T(8,128)(2,1)}) custom-call(s32[2]{0:T(128)} %pad_add_fusion.ids, bf16[1024,256]{1,0:T(8,128)(2,1)} %get-tuple-element.102.refs_0_, bf16[1024,256]{1,0:T(8,128)(2,1)} %collective-permute-done.refs_1_, bf16[1024,256]{1,0:T(8,128)(2,1)} %collective-permute-done.1.refs_2_, ...), custom_call_target="tpu_custom_call" | custom-call | flops 22000001024 | bytes 12000000 | tf_op jit(solution)/shard_map/attention/pallas_call | solution.py:605
  96.6 22.9 %attention.3 = (bf16[512,1024]{1,0:T(8,128)(2,1)}, bf16[512,1024]{1,0:T(8,128)(2,1)}) custom-call(s32[2]{0:T(128)} %pad_add_fusion.ids, bf16[1024,256]{1,0:T(8,128)(2,1)} %get-tuple-element.102.refs_0_, bf16[1024,256]{1,0:T(8,128)(2,1)} %collective-permute-done.refs_1_, bf16[1024,256]{1,0:T(8,128)(2,1)} %collective-permute-done.1.refs_2_, ...), custom_call_target="tpu_custom_call" | custom-call | flops 22000001024 | bytes 12000000 | tf_op jit(solution)/shard_map/attention/pallas_call | solution.py:605
  120.2 23.1 %attention.5 = (bf16[256,1024]{1,0:T(8,128)(2,1)}, bf16[256,1024]{1,0:T(8,128)(2,1)}, bf16[256,1024]{1,0:T(8,128)(2,1)}, bf16[256,1024]{1,0:T(8,128)(2,1)}) custom-call(s32[2]{0:T(128)} %pad_add_fusion.ids, bf16[1024,256]{1,0:T(8,128)(2,1)} %get-tuple-element.44.refs_4_.refs_0_, bf16[1024,256]{1,0:T(8,128)(2,1)} %collective-permute-done.3.refs_5_.refs_1_, ...), custom_call_target="tpu_custom_call" | custom-call | flops 22000001024 | bytes 12000000 | tf_op jit(solution)/shard_map/attention/pallas_call | solution.py:605
  148.8 9.8 %collective-permute-done.38.refs_22_ = bf16[256,1024]{1,0:T(8,128)(2,1)} collective-permute-done((bf16[256,1024]{1,0:T(8,128)(2,1)}, bf16[256,1024]{1,0:T(8,128)(2,1)}, u32[]{:S(2)}, u32[]{:S(2)}) %collective-permute-start.38) | collective-permute-done | bytes 524320 | tf_op jit(solution)/shard_map/ppermute | solution.py:1048
  160.2 8.8 %collective-permute-done.39.refs_23_ = bf16[256,1024]{1,0:T(8,128)(2,1)} collective-permute-done((bf16[256,1024]{1,0:T(8,128)(2,1)}, bf16[256,1024]{1,0:T(8,128)(2,1)}, u32[]{:S(2)}, u32[]{:S(2)}) %collective-permute-start.39) | collective-permute-done | bytes 524320 | tf_op jit(solution)/shard_map/ppermute | solution.py:1048
  169.0 25.1 %finish_attention.1 = (f32[768,1024]{1,0:T(8,128)}, f32[768,1024]{1,0:T(8,128)}, f32[128,6144]{1,0:T(8,128)}, f32[8,1024]{1,0:T(8,128)}) custom-call(s32[2]{0:T(128)} %pad_add_fusion.ids, bf16[1024,256]{1,0:T(8,128)(2,1)} %get-tuple-element.102.refs_0_, bf16[1024,256]{1,0:T(8,128)(2,1)} %collective-permute-done.refs_1_, ...), custom_call_target="tpu_custom_call" | custom-call | flops 17999998976 | bytes 30000000 | tf_op jit(solution)/shard_map/finish_attention/pallas_call | solution.py:745
  205.1 19.5 %collective-permute-done.17.refs_22_ = bf16[2048,256]{1,0:T(8,128)(2,1)S(1)} collective-permute-done((bf16[2048,256]{1,0:T(8,128)(2,1)}, bf16[2048,256]{1,0:T(8,128)(2,1)S(1)}, u32[]{:S(2)}, u32[]{:S(2)}) %collective-permute-start.17) | collective-permute-done | bytes 1048608 | tf_op jit(solution)/shard_map/ppermute | solution.py:1048
  230.5 8.5 %collective-permute-done.18.refs_23_ = bf16[1024,256]{1,0:T(8,128)(2,1)S(1)} collective-permute-done((bf16[1024,256]{1,0:T(8,128)(2,1)S(1)}, bf16[1024,256]{1,0:T(8,128)(2,1)S(1)}, u32[]{:S(2)}, u32[]{:S(2)}) %collective-permute-start.18) | collective-permute-done | bytes 524320 | tf_op jit(solution)/shard_map/ppermute | solution.py:1048
  243.2 39.5 %mlp_first.1 = (bf16[768,4096]{1,0:T(8,128)(2,1)}, bf16[768,4096]{1,0:T(8,128)(2,1)}, bf16[768,128]{1,0:T(8,128)(2,1)}, bf16[768,128]{1,0:T(8,128)(2,1)}, f32[128,10240]{1,0:T(8,128)}) custom-call(s32[2]{0:T(128)} %pad_add_fusion.ids, bf16[1024,256]{1,0:T(8,128)(2,1)} %get-tuple-element.102.refs_0_, bf16[1024,256]{1,0:T(8,128)(2,1)} %collective-permute-done.refs_1_, ...), custom_call_target="tpu_custom_call" | custom-call | flops 28000000000 | bytes 40000000 | tf_op jit(solution)/shard_map/mlp_first/pallas_call | solution.py:887
  290.0 29.7 %mlp_second.1 = (bf16[768,256]{1,0:T(8,128)(2,1)}, bf16[768,256]{1,0:T(8,128)(2,1)}, bf16[768,256]{1,0:T(8,128)(2,1)}, bf16[768,256]{1,0:T(8,128)(2,1)}, f32[768...) custom-call(s32[2]{0:T(128)} %pad_add_fusion.ids, ...), custom_call_target="tpu_custom_call" | custom-call | flops 20000000000 | bytes 45000000 | tf_op jit(solution)/shard_map/mlp_second/pallas_call | solution.py:975
  328.0 15.5 %collective-permute-done.58 = bf16[32,10240]{1,0:T(8,128)(2,1)S(1)} collective-permute-done((bf16[32,10240]{1,0:T(8,128)(2,1)S(1)}, bf16[32,10240]{1,0:T(8,128)(2,1)S(1)}, u32[]{:S(2)}, u32[]{:S(2)}) %collective-permute-start.58) | collective-permute-done | bytes 655392 | tf_op jit(solution)/shard_map/ppermute | solution.py:1048
  350.3 8.9 %collective-permute-done.59 = bf16[16,10240]{1,0:T(8,128)(2,1)S(1)} collective-permute-done((bf16[16,10240]{1,0:T(8,128)(2,1)S(1)}, bf16[16,10240]{1,0:T(8,128)(2,1)S(1)}, u32[]{:S(2)}, u32[]{:S(2)}) %collective-permute-start.59) | collective-permute-done | bytes 327712 | tf_op jit(solution)/shard_map/ppermute | solution.py:1048
  359.5 8.7 %collective-permute-done.60 = bf16[8,10240]{1,0:T(8,128)(2,1)S(1)} collective-permute-done((bf16[8,10240]{1,0:T(8,128)(2,1)S(1)}, bf16[8,10240]{1,0:T(8,128)(2,1)S(1)}, u32[]{:S(2)}, u32[]{:S(2)}) %collective-permute-start.60) | collective-permute-done | bytes 163872 | tf_op jit(solution)/shard_map/ppermute | solution.py:1048
  387.1 6.2 %collective-permute-done.53 = bf16[8,6144]{1,0:T(8,128)(2,1)S(1)} collective-permute-done((bf16[8,6144]{1,0:T(8,128)(2,1)S(1)}, bf16[8,6144]{1,0:T(8,128)(2,1)S(1)}, u32[]{:S(2)}, u32[]{:S(2)}) %collective-permute-start.53) | collective-permute-done | bytes 98336 | tf_op jit(solution)/shard_map/ppermute | solution.py:1048
  393.3 7.2 %collective-permute-done.63 = bf16[8,10240]{1,0:T(8,128)(2,1)S(1)} collective-permute-done((bf16[8,10240]{1,0:T(8,128)(2,1)S(1)}, bf16[8,10240]{1,0:T(8,128)(2,1)S(1)}, u32[]{:S(2)}, u32[]{:S(2)}) %collective-permute-start.63) | collective-permute-done | bytes 163872 | tf_op jit(solution)/shard_map/ppermute | solution.py:1048
  400.6 5.6 %collective-permute-done.54 = bf16[16,6144]{1,0:T(8,128)(2,1)S(1)} collective-permute-done((bf16[16,6144]{1,0:T(8,128)(2,1)S(1)}, bf16[16,6144]{1,0:T(8,128)(2,1)S(1)}, u32[]{:S(2)}, u32[]{:S(2)}) %collective-permute-start.54) | collective-permute-done | bytes 196640 | tf_op jit(solution)/shard_map/ppermute | solution.py:1048
  414.5 10.8 %collective-permute-done.55 = bf16[32,6144]{1,0:T(8,128)(2,1)S(1)} collective-permute-done((bf16[32,6144]{1,0:T(8,128)(2,1)S(1)}, bf16[32,6144]{1,0:T(8,128)(2,1)S(1)}, u32[]{:S(2)}, u32[]{:S(2)}) %collective-permute-start.55) | collective-permute-done | bytes 393248 | tf_op jit(solution)/shard_map/ppermute | solution.py:1048
  427.7 8.2 %collective-permute-done.65 = bf16[32,10240]{1,0:T(8,128)(2,1)S(1)} collective-permute-done((bf16[32,10240]{1,0:T(8,128)(2,1)S(1)}, bf16[32,10240]{1,0:T(8,128)(2,1)S(1)}, u32[]{:S(2)}, u32[]{:S(2)}) %collective-permute-start.65) | collective-permute-done | bytes 655392 | tf_op jit(solution)/shard_map/ppermute | solution.py:1048
  437.4 39.4 %psum.7 = f32[4,1024]{1,0:T(4,128)S(1)} all-reduce(f32[4,1024]{1,0:T(4,128)S(1)} %pad_maximum_fusion.9), channel_id=1, replica_groups=mesh['dp'=8,'mp'=4] {'dp','mp'}, use_global_device_ids=true, to_apply=%region_0.1 | all-reduce | flops 4096 | bytes 32768 | tf_op jit(solution)/shard_map/psum | solution.py:1189
  (286 shorter events, 141.3 us)
Async XLA Ops:
  7.8 26.9 %collective-permute-start = (bf16[1024,256]{1,0:T(8,128)(2,1)}, bf16[1024,256]{1,0:T(8,128)(2,1)}, u32[]{:S(2)}, u32[]{:S(2)}) collective-permute-start(bf16[1024,256]{1,0:T(8,128)(2,1)} %get-tuple-element.102.refs_0_), channel_id=1, source_target_pairs={{0,1},{1,0},{2,3},{3,2},{4,5},{5,4},{6,7},{7,6},{8,9},{9,8},{10,11... | collective-permute-start | bytes 1572872 | tf_op jit(solution)/shard_map/ppermute | solution.py:1048
  9.1 28.7 %collective-permute-start.6 = (bf16[1024,256]{1,0:T(8,128)(2,1)S(1)}, bf16[1024,256]{1,0:T(8,128)(2,1)}, u32[]{:S(2)}, u32[]{:S(2)}) collective-permute-start(bf16[1024,256]{1,0:T(8,128)(2,1)S(1)} %get-tuple-element.96.refs_8_.refs_4_), channel_id=1, source_target_pairs={{0,1},{1,0},{2,3},{3,2},{4,5},{5,4},{6,7},{7,6},{8,9},{9,8},{10,11... | collective-permute-start | bytes 1572872 | tf_op jit(solution)/shard_map/ppermute | solution.py:1048
  64.1 55.4 %collective-permute-start.3 = (bf16[1024,256]{1,0:T(8,128)(2,1)S(1)}, bf16[1024,256]{1,0:T(8,128)(2,1)}, u32[]{:S(2)}, u32[]{:S(2)}) collective-permute-start(bf16[1024,256]{1,0:T(8,128)(2,1)S(1)} %copy-done.10), channel_id=1, source_target_pairs={{0,1},{1,0},{2,3},{3,2},{4,5},{5,4},{6,7},{7,6},{8,9},{9,8},{10,11... | collective-permute-start | bytes 1572872 | tf_op jit(solution)/shard_map/ppermute | solution.py:1048
  71.5 48.2 %collective-permute-start.10 = (bf16[1024,256]{1,0:T(8,128)(2,1)}, bf16[1024,256]{1,0:T(8,128)(2,1)}, u32[]{:S(2)}, u32[]{:S(2)}) collective-permute-start(bf16[1024,256]{1,0:T(8,128)(2,1)} %get-tuple-element.46.refs_12_.refs_4_), channel_id=1, source_target_pairs={{0,1},{1,0},{2,3},{3,2},{4,5},{5,4},{6,7},{7,6},{8,9},{9,8},{10,11... | collective-permute-start | bytes 1572872 | tf_op jit(solution)/shard_map/ppermute | solution.py:1048
  71.5 73.6 %collective-permute-start.40 = (bf16[1024,768]{1,0:T(8,128)(2,1)}, bf16[1024,768]{1,0:T(8,128)(2,1)}, u32[]{:S(2)}, u32[]{:S(2)}) collective-permute-start(bf16[1024,768]{1,0:T(8,128)(2,1)} %refs_24_.1), channel_id=1, source_target_pairs={{0,1},{1,0},{2,3},{3,2},{4,5},{5,4},{6,7},{7,6},{8,9},{9,8},{10,11... | collective-permute-start | bytes 4718600 | tf_op jit(solution)/shard_map/ppermute | solution.py:1048
  72.1 48.1 %collective-permute-start.5 = (bf16[1024,256]{1,0:T(8,128)(2,1)}, bf16[1024,256]{1,0:T(8,128)(2,1)}, u32[]{:S(2)}, u32[]{:S(2)}) collective-permute-start(bf16[1024,256]{1,0:T(8,128)(2,1)} %copy-done.33), channel_id=1, source_target_pairs={{0,1},{1,0},{2,3},{3,2},{4,5},{5,4},{6,7},{7,6},{8,9},{9,8},{10,11... | collective-permute-start | bytes 1572872 | tf_op jit(solution)/shard_map/ppermute | solution.py:1048
  72.9 47.3 %collective-permute-start.12 = (bf16[1024,256]{1,0:T(8,128)(2,1)}, bf16[1024,256]{1,0:T(8,128)(2,1)}, u32[]{:S(2)}, u32[]{:S(2)}) collective-permute-start(bf16[1024,256]{1,0:T(8,128)(2,1)} %collective-permute-done.11.refs_14_.refs_6_), channel_id=1, source_target_pairs={{0,1},{1,0},{2,3},{3,2},{4,5},{5,4},{6,7},{7,6},{8,9},{9,8},{10,11... | collective-permute-start | bytes 1572872 | tf_op jit(solution)/shard_map/ppermute | solution.py:1048
  119.5 28.7 %collective-permute-start.36 = (bf16[512,1024]{1,0:T(8,128)(2,1)}, bf16[512,1024]{1,0:T(8,128)(2,1)}, u32[]{:S(2)}, u32[]{:S(2)}) collective-permute-start(bf16[512,1024]{1,0:T(8,128)(2,1)} %get-tuple-element.53), channel_id=1, source_target_pairs={{0,1},{1,0},{2,3},{3,2},{4,5},{5,4},{6,7},{7,6},{8,9},{9,8},{10,11... | collective-permute-start | bytes 3145736 | tf_op jit(solution)/shard_map/ppermute | solution.py:1048
  119.8 49.2 %collective-permute-start.35 = (bf16[512,1024]{1,0:T(8,128)(2,1)}, bf16[512,1024]{1,0:T(8,128)(2,1)}, u32[]{:S(2)}, u32[]{:S(2)}) collective-permute-start(bf16[512,1024]{1,0:T(8,128)(2,1)} %get-tuple-element.51), channel_id=1, source_target_pairs={{0,1},{1,0},{2,3},{3,2},{4,5},{5,4},{6,7},{7,6},{8,9},{9,8},{10,11... | collective-permute-start | bytes 3145736 | tf_op jit(solution)/shard_map/ppermute | solution.py:1048
  148.3 78.2 %collective-permute-start.14 = (bf16[4096,256]{1,0:T(8,128)(2,1)}, bf16[4096,256]{1,0:T(8,128)(2,1)}, u32[]{:S(2)}, u32[]{:S(2)}) collective-permute-start(bf16[4096,256]{1,0:T(8,128)(2,1)} %refs_18_.3), channel_id=1, source_target_pairs={{0,1},{1,0},{2,3},{3,2},{4,5},{5,4},{6,7},{7,6},{8,9},{9,8},{10,11... | collective-permute-start | bytes 6291464 | tf_op jit(solution)/shard_map/ppermute | solution.py:1048
  148.7 78.5 %collective-permute-start.13 = (bf16[1024,1024]{1,0:T(8,128)(2,1)}, bf16[1024,1024]{1,0:T(8,128)(2,1)}, u32[]{:S(2)}, u32[]{:S(2)}) collective-permute-start(bf16[1024,1024]{1,0:T(8,128)(2,1)} %refs_16_.3), channel_id=1, source_target_pairs={{0,1},{1,0},{2,3},{3,2},{4,5},{5,4},{6,7},{7,6},{8,9},{9,8},{10,11... | collective-permute-start | bytes 6291464 | tf_op jit(solution)/shard_map/ppermute | solution.py:1048
  158.6 40.5 %collective-permute-start.15 = (bf16[2048,256]{1,0:T(8,128)(2,1)}, bf16[2048,256]{1,0:T(8,128)(2,1)}, u32[]{:S(2)}, u32[]{:S(2)}) collective-permute-start(bf16[2048,256]{1,0:T(8,128)(2,1)} %dynamic-slice_dynamic-update-slice_fusion), channel_id=1, source_target_pairs={{0,2},{1,3},{2,0},{3,1},{4,6},{5,7},{6,4},{7,5},{8,10},{9,11},{10,... | collective-permute-start | bytes 3145736 | tf_op jit(solution)/shard_map/ppermute | solution.py:1048
  195.6 31.6 %collective-permute-start.47 = (f32[64,6144]{1,0:T(8,128)S(1)}, f32[64,6144]{1,0:T(8,128)S(1)}, u32[]{:S(2)}, u32[]{:S(2)}) collective-permute-start(f32[64,6144]{1,0:T(8,128)S(1)} %constant_dynamic-slice_fusion.4), channel_id=1, source_target_pairs={{0,1},{1,0},{2,3},{3,2},{4,5},{5,4},{6,7},{7,6},{8,9},{9,8},{10,11... | collective-permute-start | bytes 4718600 | tf_op jit(solution)/shard_map/ppermute | solution.py:1048
  239.7 46.7 %collective-permute-start.48 = (bf16[32,6144]{1,0:T(8,128)(2,1)S(1)}, bf16[32,6144]{1,0:T(8,128)(2,1)}, u32[]{:S(2)}, u32[]{:S(2)}) collective-permute-start(bf16[32,6144]{1,0:T(8,128)(2,1)S(1)} %dynamic-slice_convert_fusion.1), channel_id=1, source_target_pairs={{0,4},{4,0},{8,12},{12,8},{16,20},{20,16},{24,28},{28,24},{1,5},{5... | collective-permute-start | bytes 1179656 | tf_op jit(solution)/shard_map/ppermute | solution.py:1048
  286.1 37.7 %collective-permute-start.57 = (f32[64,10240]{1,0:T(8,128)}, f32[64,10240]{1,0:T(8,128)}, u32[]{:S(2)}, u32[]{:S(2)}) collective-permute-start(f32[64,10240]{1,0:T(8,128)} %constant_dynamic-slice_fusion.2), channel_id=1, source_target_pairs={{0,1},{1,0},{2,3},{3,2},{4,5},{5,4},{6,7},{7,6},{8,9},{9,8},{10,11... | collective-permute-start | bytes 7864328 | tf_op jit(solution)/shard_map/ppermute | solution.py:1048
  288.3 34.0 %collective-permute-start.49 = (bf16[16,6144]{1,0:T(8,128)(2,1)S(1)}, bf16[16,6144]{1,0:T(8,128)(2,1)S(1)}, u32[]{:S(2)}, u32[]{:S(2)}) collective-permute-start(bf16[16,6144]{1,0:T(8,128)(2,1)S(1)} %dynamic-slice_convert_fusion.3), channel_id=1, source_target_pairs={{0,8},{4,12},{8,0},{12,4},{16,24},{20,28},{24,16},{28,20},{1,9},{5... | collective-permute-start | bytes 589832 | tf_op jit(solution)/shard_map/ppermute | solution.py:1048
  320.5 106.8 %collective-permute-start.41 = (bf16[768,256]{1,0:T(8,128)(2,1)}, bf16[768,256]{1,0:T(8,128)(2,1)S(1)}, u32[]{:S(2)}, u32[]{:S(2)}) collective-permute-start(bf16[768,256]{1,0:T(8,128)(2,1)} %get-tuple-element.63), channel_id=1, source_target_pairs={{0,1},{1,0},{2,3},{3,2},{4,5},{5,4},{6,7},{7,6},{8,9},{9,8},{10,11... | collective-permute-start | bytes 1179656 | tf_op jit(solution)/shard_map/ppermute | solution.py:1048
  320.5 106.7 %collective-permute-start.42 = (bf16[768,256]{1,0:T(8,128)(2,1)}, bf16[768,256]{1,0:T(8,128)(2,1)S(1)}, u32[]{:S(2)}, u32[]{:S(2)}) collective-permute-start(bf16[768,256]{1,0:T(8,128)(2,1)} %get-tuple-element.64), channel_id=1, source_target_pairs={{0,2},{1,3},{2,0},{3,1},{4,6},{5,7},{6,4},{7,5},{8,10},{9,11},{10,... | collective-permute-start | bytes 1179656 | tf_op jit(solution)/shard_map/ppermute | solution.py:1048
  321.9 114.2 %collective-permute-start.43 = (bf16[768,256]{1,0:T(8,128)(2,1)}, bf16[768,256]{1,0:T(8,128)(2,1)S(1)}, u32[]{:S(2)}, u32[]{:S(2)}) collective-permute-start(bf16[768,256]{1,0:T(8,128)(2,1)} %get-tuple-element.65), channel_id=1, source_target_pairs={{0,3},{1,2},{2,1},{3,0},{4,7},{5,6},{6,5},{7,4},{8,11},{9,10},{10,... | collective-permute-start | bytes 1179656 | tf_op jit(solution)/shard_map/ppermute | solution.py:1048
  322.4 157.5 %collective-permute-start.45 = (bf16[768,256]{1,0:T(8,128)(2,1)}, bf16[768,256]{1,0:T(8,128)(2,1)S(1)}, u32[]{:S(2)}, u32[]{:S(2)}) collective-permute-start(bf16[768,256]{1,0:T(8,128)(2,1)} %get-tuple-element.68), channel_id=1, source_target_pairs={{0,2},{1,3},{2,0},{3,1},{4,6},{5,7},{6,4},{7,5},{8,10},{9,11},{10,... | collective-permute-start | bytes 1179656 | tf_op jit(solution)/shard_map/ppermute | solution.py:1048
  427.3 52.6 %collective-permute-start.46 = (bf16[768,256]{1,0:T(8,128)(2,1)}, bf16[768,256]{1,0:T(8,128)(2,1)}, u32[]{:S(2)}, u32[]{:S(2)}) collective-permute-start(bf16[768,256]{1,0:T(8,128)(2,1)} %get-tuple-element.69), channel_id=1, source_target_pairs={{0,3},{1,2},{2,1},{3,0},{4,7},{5,6},{6,5},{7,4},{8,11},{9,10},{10,... | collective-permute-start | bytes 1179656 | tf_op jit(solution)/shard_map/ppermute | solution.py:1048
  427.3 52.6 %collective-permute-start.44 = (f32[768,256]{1,0:T(8,128)}, f32[768,256]{1,0:T(8,128)}, u32[]{:S(2)}, u32[]{:S(2)}) collective-permute-start(f32[768,256]{1,0:T(8,128)} %get-tuple-element.67), channel_id=1, source_target_pairs={{0,1},{1,0},{2,3},{3,2},{4,5},{5,4},{6,7},{7,6},{8,9},{9,8},{10,11... | collective-permute-start | bytes 2359304 | tf_op jit(solution)/shard_map/ppermute | solution.py:1048
  435.8 48.2 %collective-permute-start.56 = (bf16[64,6144]{1,0:T(8,128)(2,1)}, bf16[64,6144]{1,0:T(8,128)(2,1)}, u32[]{:S(2)}, u32[]{:S(2)}) collective-permute-start(bf16[64,6144]{1,0:T(8,128)(2,1)} %maximum_select_fusion.3), channel_id=1, source_target_pairs={{0,1},{1,0},{2,3},{3,2},{4,5},{5,4},{6,7},{7,6},{8,9},{9,8},{10,11... | collective-permute-start | bytes 2359304 | tf_op jit(solution)/shard_map/ppermute | solution.py:1048
  436.8 53.6 %collective-permute-start.66 = (bf16[64,10240]{1,0:T(8,128)(2,1)S(1)}, bf16[64,10240]{1,0:T(8,128)(2,1)}, u32[]{:S(2)}, u32[]{:S(2)}) collective-permute-start(bf16[64,10240]{1,0:T(8,128)(2,1)S(1)} %maximum_select_fusion.2), channel_id=1, source_target_pairs={{0,1},{1,0},{2,3},{3,2},{4,5},{5,4},{6,7},{7,6},{8,9},{9,8},{10,11... | collective-permute-start | bytes 3932168 | tf_op jit(solution)/shard_map/ppermute | solution.py:1048
  (87 other events, 1113.2 us)
